TPU v7x, 32 devices: a whole 2x2x4 slice. The times are simulated.
32 devices in a mesh: seq: 8 (over z, y), head: 4 (over x, core).
Axes of the slice: x: 2, y: 2, z: 4, core: 2. Of those that a mesh axis runs over, the one named last changes fastest.
Arguments:
- queries: bfloat16 [1024, 4096], P('seq', 'head'), may hold values from -6 to 6
- key_rows: bfloat16 [1024, 4096], P('seq', 'head'), may hold values from -6 to 6
- value_rows: bfloat16 [1024, 4096], P('seq', 'head'), may hold values from -6 to 6
- log_decay: float32 [32, 1024], P('head', 'seq'), may hold values from -3 to 0
- init_state: float32 [32, 128, 128], P('head'), may hold values from -48 to 48
- attn_gain: float32 [4096], P('head'), may hold values from 0.1 to 1.9
- out_weight: bfloat16 [4096, 6144], P('head', 'seq'), may hold values from -0.09375 to 0.09375
- residual: bfloat16 [1024, 6144], P('seq', 'head'), may hold values from -13 to 13
- ffn_gain: float32 [6144], replicated, may hold values from 0.1 to 1.9
- router: float32 [6144, 8], replicated, may hold values from -0.078125 to 0.078125
- expert_ids: int32 [1024, 2], P('seq'), may hold values from 0 to 7, all different within a row; in each aligned block of 128 rows (0 to 127, 128 to 255, ...) at most 64 rows name the same one
- gate_weight: bfloat16 [8, 6144, 4608], P('seq', None, 'head'), may hold values from -0.078125 to 0.078125
- up_weight: bfloat16 [8, 6144, 4608], P('seq', None, 'head'), may hold values from -0.078125 to 0.078125
- down_weight: bfloat16 [8, 4608, 6144], P('seq', 'head'), may hold values from -0.09375 to 0.09375
Outputs:
- output: bfloat16 [1024, 6144], P('seq', 'head')
Inputs may be any that keep to these rules, and one draw needn't show every extreme that they name: `expert_ids`: the two ids of a row differ. In each aligned block of 128 rows no expert is named more than 64 times, a bound that some block reaches.
All inputs are finite; a program needn't handle non-finite values.
Results may differ from a plain program's by a relative error of at most 0.018.
Values may be sent and summed in bfloat16 or wider, within the bound.
A program may use at most 128 MiB of HBM per device.

v0:
```python
import jax
import jax.numpy as jnp
from jax import lax
from jax.sharding import PartitionSpec as P

D = 6144
HEAD_DIM = 128


epsilon = 1e-06
highest = lax.Precision.HIGHEST


def prefix(x, axis, combine, identity):
    size, place = (lax.axis_size(axis), lax.axis_index(axis))
    everything = jax.tree.map(
        lambda part, kind: lax.all_gather(part.astype(kind), axis), x, (jnp.bfloat16, jnp.bfloat16)
    )
    start = jax.tree.map(
        lambda part, zero: jnp.broadcast_to(jnp.asarray(zero, part.dtype), part.shape), x, identity
    )

    def turn(k, before):
        reached = k < place
        new = combine(
            before, jax.tree.map(lambda part, own: part[k].astype(own.dtype), everything, x)
        )
        return jax.tree.map(lambda a, b: jnp.where(reached, a, b), new, before)

    return lax.fori_loop(0, size, turn, start)


def block_attend(query_block, key_block, value_block, cumulative, entering):
    length = cumulative.shape[1]
    causal = jnp.arange(length)[:, None] >= jnp.arange(length)[None, :]
    spread = jnp.where(causal[None], cumulative[:, :, None] - cumulative[:, None, :], 0.0)
    fading = jnp.where(causal[None], jnp.exp(spread), 0.0)
    scores = jnp.einsum("thd,shd->hts", query_block, key_block, preferred_element_type=jnp.float32)
    weights = (fading * scores).astype(jnp.bfloat16)
    within = jnp.einsum("hts,shd->thd", weights, value_block, preferred_element_type=jnp.float32)
    carried = jnp.einsum(
        "thd,hde->the", query_block.astype(jnp.float32), entering, precision=highest
    )
    return within + jnp.exp(cumulative).T[:, :, None] * carried


def block_state(key_block, value_block, cumulative):
    remain = jnp.exp(cumulative[:, -1:] - cumulative)
    return jnp.einsum(
        "shd,hs,she->hde",
        key_block.astype(jnp.float32),
        remain,
        value_block.astype(jnp.float32),
        precision=highest,
    )


def join_states(earlier, latter):
    return (earlier[0] + latter[0], jnp.exp(latter[0])[:, None, None] * earlier[1] + latter[1])


def on_device(
    queries,
    key_rows,
    value_rows,
    log_decay,
    init_state,
    attn_gain,
    out_weight,
    residual,
    ffn_gain,
    router,
    expert_ids,
    gate_weight,
    up_weight,
    down_weight,
):
    tokens_here = queries.shape[0]
    heads_here = log_decay.shape[0]
    shaped = (tokens_here, heads_here, HEAD_DIM)
    query_heads = queries.reshape(shaped)
    key_heads = key_rows.reshape(shaped)
    value_heads = value_rows.reshape(shaped)
    cumulative = jnp.cumsum(log_decay, axis=1)
    block_decay = cumulative[:, -1]
    local_state = block_state(key_heads, value_heads, cumulative)
    identity = (jnp.zeros_like(block_decay), jnp.zeros_like(local_state))
    prior_decay, prior_state = prefix((block_decay, local_state), "seq", join_states, identity)
    entering = jnp.exp(prior_decay)[:, None, None] * init_state + prior_state
    attended = block_attend(query_heads, key_heads, value_heads, cumulative, entering)
    inverse = lax.rsqrt(jnp.mean(attended * attended, axis=-1, keepdims=True) + epsilon)
    attn_rows = (
        (attended * inverse * attn_gain.reshape(heads_here, HEAD_DIM))
        .reshape(tokens_here, heads_here * HEAD_DIM)
        .astype(jnp.bfloat16)
    )
    projected = jnp.dot(
        attn_rows,
        lax.all_gather(out_weight, "seq", axis=1, tiled=True),
        preferred_element_type=jnp.float32,
    )
    width_here = residual.shape[1]
    first_column = lax.axis_index("head") * width_here
    own_columns = lax.dynamic_slice_in_dim(
        projected, first_column, width_here, 1
    ) + residual.astype(jnp.float32)
    projected = lax.dynamic_update_slice_in_dim(projected, own_columns, first_column, 1)
    experts = router.shape[1]
    stream_here = lax.psum_scatter(
        projected.astype(jnp.bfloat16), "head", scatter_dimension=1, tiled=True
    ).astype(jnp.float32)
    gain_here = lax.dynamic_slice_in_dim(ffn_gain, first_column, width_here, 0)
    router_here = lax.dynamic_slice_in_dim(router, first_column, width_here, 0)
    weighted = stream_here * gain_here
    squares, partial_logits = lax.psum(
        (
            jnp.sum(stream_here * stream_here, axis=-1),
            jnp.dot(weighted, router_here, precision=highest),
        ),
        "head",
    )
    inverse_rms = lax.rsqrt(squares / D + epsilon)[:, None]
    normed = weighted * inverse_rms
    logits = partial_logits * inverse_rms
    expert_in = normed.astype(jnp.bfloat16)
    matches = expert_ids[:, :, None] == jnp.arange(experts)[None, None, :]
    chosen = jnp.sum(jnp.where(matches, logits[:, None, :], 0.0), axis=-1)
    gate_share = jax.nn.sigmoid(chosen - chosen[:, ::-1])
    capacity = 4 * tokens_here // experts
    flat_hits = matches.reshape(tokens_here * 2, experts).astype(jnp.int32)
    position = jnp.sum(jnp.cumsum(flat_hits, axis=0) * flat_hits, axis=1) - 1
    slot_index = expert_ids.reshape(-1) * capacity + position
    target = slot_index[None, :] == jnp.arange(experts * capacity)[:, None]
    source = jnp.sum(jnp.where(target, jnp.arange(tokens_here * 2)[None, :] // 2, 0), axis=1)
    filled = jnp.any(target, axis=1)
    outgoing = jnp.where(filled[:, None], expert_in[source], jnp.zeros((), jnp.bfloat16)).reshape(
        experts, capacity, -1
    )
    gate_here = gate_weight[0]
    up_here = up_weight[0]
    down_here = down_weight[0]
    arrived = lax.all_to_all(outgoing, "seq", split_axis=0, concat_axis=0, tiled=True)
    sources, slot_count, columns = arrived.shape
    flat_rows = arrived.reshape(sources * slot_count, columns)
    portion = lax.all_gather(flat_rows, "head", axis=1, tiled=True)
    gate_act = jnp.dot(portion, gate_here, preferred_element_type=jnp.float32)
    up_act = jnp.dot(portion, up_here, preferred_element_type=jnp.float32)
    hidden = (jax.nn.silu(gate_act) * up_act).astype(jnp.bfloat16)
    partial_value = jnp.dot(hidden, down_here, preferred_element_type=jnp.float32)
    summed = lax.psum_scatter(
        partial_value.astype(jnp.bfloat16), "head", scatter_dimension=1, tiled=True
    )
    returning = summed.reshape(sources, slot_count, -1)
    returned = lax.all_to_all(returning, "seq", split_axis=0, concat_axis=0, tiled=True)
    flat_back = returned.reshape(experts * capacity, -1)
    picked = flat_back[slot_index].reshape(tokens_here, 2, -1).astype(jnp.float32)
    mixture = jnp.sum(gate_share[:, :, None] * picked, axis=1)
    return (stream_here + mixture).astype(jnp.bfloat16)


def solution(mesh):
    return jax.shard_map(
        on_device,
        mesh=mesh,
        in_specs=(
            P("seq", "head"),
            P("seq", "head"),
            P("seq", "head"),
            P("head", "seq"),
            P("head", None, None),
            P("head"),
            P("head", "seq"),
            P("seq", "head"),
            P(),
            P(),
            P("seq", None),
            P("seq", None, "head"),
            P("seq", None, "head"),
            P("seq", "head", None),
        ),
        out_specs=P("seq", "head"),
        check_vma=False,
    )
```

profile of v0, /device:TPU:0, one launch (start us, length us, event | category | flops | bytes accessed | tf_op | source)
XLA Modules:
  0.0 520.5 jit_solution(8868768714697688793)
XLA Ops:
  6.5 1.0 reduce_window_sum.26
  7.8 1.1 copy.60
  12.8 23.2 %all-reduce = bf16[64]{0:T(256)(128)(2,1)S(1)} all-reduce(bf16[64]{0:T(256)(128)(2,1)S(1)} %dynamic-update-slice), channel_id=2, replica_groups=mesh['seq'=8,'head'=4] {'seq'}, use_global_device_ids=true, to_apply=%add | all-reduce | flops 64 | bytes 256
  36.1 26.4 %all-gather.10.cloned.1.call-done = bf16[64,128,128]{2,1,0:T(8,128)(2,1)} async-done(((bf16[8,128,128]{2,1,0:T(8,128)(2,1)}), bf16[64,128,128]{2,1,0:T(8,128)(2,1)}) %all-gather.10.cloned.1.call-update) | async-done | bytes 2097168 | tf_op jit(solution)/shard_map/all_gather | solution.py:17
  62.5 9.2 %while.16 = (s32[]{:T(128)}, f32[8]{0:T(128)S(1)}, f32[8,128,128]{2,1,0:T(8,128)S(1)}, s32[]{:T(128)}, bf16[8,8]{1,0:T(8,128)(2,1)S(1)}, /*index=5*/bf16[8,8,128,128]{3,2,1,0:T(8,128)(2,1)}, s32[]{:T(128)}, s32[]{:T(128)}) while((s32[]{:T(128)}, f32[8]{0:T(128)S(1)}, f32[8,128,128]{2,1,0:T(8,128)S(1)}, s32[]{:T(128)}, ...), condition=%wide.region_2.3_spmd.clone, body=%wide.region_1.2_spmd.clone.sunk | while | flops 655396 | bytes 1310979 | solution.py:30
  62.5 1.2 fusion.75
  63.7 1.1 fusion.75
  64.8 1.1 fusion.75
  66.0 1.1 fusion.75
  67.1 1.1 fusion.75
  68.3 1.1 fusion.75
  69.4 1.1 fusion.75
  70.6 1.1 fusion.75
  73.2 166.2 %all-gather.6.cloned.1.call-done = bf16[1024,6144]{1,0:T(8,128)(2,1)} async-done(((bf16[1024,768]{1,0:T(8,128)(2,1)}), bf16[1024,6144]{1,0:T(8,128)(2,1)}) %all-gather.6.cloned.1.call-update) | async-done | bytes 12582928 | tf_op jit(solution)/shard_map/all_gather | solution.py:99
  239.4 6.7 %fusion.63 = f32[128,6144]{1,0:T(8,128)S(1)} fusion(bf16[128,1024]{0,1:T(8,128)(2,1)S(1)} %bitcast.101, bf16[1024,6144]{1,0:T(8,128)(2,1)} %all-gather.6.cloned.1.call-done), kind=kOutput, calls=%fused_computation.96 | convolution fusion | flops 1610612736 | bytes 15990784 | tf_op jit(solution)/shard_map/dot_general | solution.py:97
  246.2 1.3 convert_element_type.97
  250.2 23.9 %reduce-scatter.3.cloned.1.call-done = bf16[128,1536]{1,0:T(8,128)(2,1)} async-done(((bf16[128,6144]{1,0:T(8,128)(2,1)}), bf16[128,1536]{1,0:T(8,128)(2,1)}) %reduce-scatter.3.cloned.1.call-update) | async-done | bytes 393232 | tf_op jit(solution)/shard_map/reduce_scatter | solution.py:109
  274.1 1.2 fusion.23
  275.3 1.7 fusion.21
  277.0 5.8 %all-reduce.1 = (f32[128]{0:T(128)S(1)}, f32[128,8]{0,1:T(8,128)S(1)}) all-reduce(f32[128]{0:T(128)S(1)} %fusion.23, f32[128,8]{0,1:T(8,128)S(1)} %fusion.21), channel_id=1, replica_groups=mesh['seq'=8,'head'=4] {'head'}, use_global_device_ids=true, to_apply=%region_7.8 | all-reduce | flops 1152 | bytes 9216 | tf_op jit(solution)/shard_map/psum | solution.py:115
  282.9 1.1 fusion.22
  284.0 2.1 gather_fusion
  286.3 42.4 %all_to_all.10 = bf16[8,64,1536]{2,1,0:T(8,128)(2,1)} all-to-all(bf16[8,64,1536]{2,1,0:T(8,128)(2,1)S(1)} %broadcast_select_fusion.2), channel_id=1, replica_groups=mesh['seq'=8,'head'=4] {'seq'}, dimensions={0} | all-to-all | bytes 3145728 | tf_op jit(solution)/shard_map/all_to_all | solution.py:142
  329.0 44.3 %all-gather.8.cloned.1.call-done = bf16[512,6144]{1,0:T(8,128)(2,1)} async-done(((bf16[512,1536]{1,0:T(8,128)(2,1)}), bf16[512,6144]{1,0:T(8,128)(2,1)}) %all-gather.8.cloned.1.call-update) | async-done | bytes 6291472 | tf_op jit(solution)/shard_map/all_gather | solution.py:145
  373.3 12.6 %fusion.5 = f32[512,1152]{1,0:T(8,128)S(1)} fusion(bf16[512,6144]{1,0:T(8,128)(2,1)} %all-gather.8.cloned.1.call-done, bf16[1,6144,1152]{2,1,0:T(8,128)(2,1)} %param.27), kind=kOutput, calls=%fused_computation.12 | convolution fusion | flops 7247757312 | bytes 22806528 | tf_op jit(solution)/shard_map/dot_general | solution.py:146
  385.9 11.7 %fusion.13 = bf16[512,1152]{1,0:T(8,128)(2,1)S(1)} fusion(bf16[512,6144]{1,0:T(8,128)(2,1)S(1)} %copy-done.8, bf16[1,6144,1152]{2,1,0:T(8,128)(2,1)} %param.28, f32[512,1152]{1,0:T(8,128)S(1)} %fusion.5), kind=kOutput, calls=%fused_computation.16 | convolution fusion | flops 7251296256 | bytes 23986176 | tf_op jit(solution)/shard_map/dot_general | solution.py:147
  397.7 10.0 %fusion.7 = bf16[512,6144]{1,0:T(8,128)(2,1)} fusion(bf16[512,1152]{1,0:T(8,128)(2,1)S(1)} %fusion.13, bf16[1,1152,6144]{2,1,0:T(8,128)(2,1)S(1)} %bitcast.111), kind=kOutput, calls=%fused_computation.14 | convolution fusion | flops 7250903040 | bytes 21626880 | tf_op jit(solution)/shard_map/dot_general | solution.py:149
  407.7 58.5 %reduce-scatter.5.cloned.1.call-done = bf16[512,1536]{1,0:T(8,128)(2,1)} async-done(((bf16[512,6144]{1,0:T(8,128)(2,1)}), bf16[512,1536]{1,0:T(8,128)(2,1)}) %reduce-scatter.5.cloned.1.call-update) | async-done | bytes 1572880 | tf_op jit(solution)/shard_map/reduce_scatter | solution.py:150
  466.2 5.5 %all-to-all-start.1 = ((bf16[8,64,1536]{2,1,0:T(8,128)(2,1)}), bf16[8,64,1536]{2,1,0:T(8,128)(2,1)S(1)}, u32[]{:S(2)}, u32[]{:S(2)}) async-start(bf16[8,64,1536]{2,1,0:T(8,128)(2,1)} %bitcast.100), calls=%async_computation.3 | async-start | bytes 3145728 | tf_op jit(solution)/shard_map/all_to_all | solution.py:154
  472.2 36.5 %all-to-all-done.1 = bf16[8,64,1536]{2,1,0:T(8,128)(2,1)S(1)} async-done(((bf16[8,64,1536]{2,1,0:T(8,128)(2,1)}), bf16[8,64,1536]{2,1,0:T(8,128)(2,1)S(1)}, u32[]{:S(2)}, u32[]{:S(2)}) %all-to-all-start.1) | async-done | bytes 1572896 | tf_op jit(solution)/shard_map/all_to_all | solution.py:154
  508.7 1.3 gather_fusion.1
  511.0 2.2 multiply_reduce_fusion
  (95 shorter events, 10.5 us)
Async XLA Ops:
  6.5 2.4 copy-start
  6.5 4.5 copy-start.9
  6.5 55.9 %all-gather.10.cloned.1.call-start = ((), (), s32[]{:S(2)}) async-start(), calls=%async_computation.8 | async-start | bytes 2359296 | tf_op jit(solution)/shard_map/all_gather | solution.py:17
  10.2 229.2 %all-gather.6.cloned.1.call-start = ((), (), s32[]{:S(2)}) async-start(), calls=%async_computation.4 | async-start | bytes 14155776 | tf_op jit(solution)/shard_map/all_gather | solution.py:99
  11.0 263.1 %reduce-scatter.3.cloned.1.call-start = ((), (), s32[]{:S(2)}) async-start(), calls=%async_computation.5 | async-start | bytes 1966080 | tf_op jit(solution)/shard_map/reduce_scatter | solution.py:109
  62.5 9.3 %copy-start.3 = (f32[8,128,128]{2,1,0:T(8,128)S(1)}, f32[8,128,128]{2,1,0:T(8,128)}, u32[]{:S(2)}) copy-start(f32[8,128,128]{2,1,0:T(8,128)} %param.20) | copy-start | bytes 1572868
  62.5 9.3 %copy-start.5 = (bf16[128,1024]{1,0:T(8,128)(2,1)S(1)}, bf16[128,1024]{1,0:T(8,128)(2,1)}, u32[]{:S(2)}) copy-start(bf16[128,1024]{1,0:T(8,128)(2,1)} %param.16) | copy-start | bytes 786436
  71.7 1.2 copy-start.7
  239.4 6.7 %copy-start.4 = (bf16[128,1536]{1,0:T(8,128)(2,1)S(1)}, bf16[128,1536]{1,0:T(8,128)(2,1)}, u32[]{:S(2)}) copy-start(bf16[128,1536]{1,0:T(8,128)(2,1)} %param.23) | copy-start | bytes 1179652
  246.2 1.4 copy-start.6
  247.6 125.7 %all-gather.8.cloned.1.call-start = ((), (), s32[]{:S(2)}) async-start(), calls=%async_computation.6 | async-start | bytes 7864320 | tf_op jit(solution)/shard_map/all_gather | solution.py:145
  328.7 137.5 %reduce-scatter.5.cloned.1.call-start = ((), (), s32[]{:S(2)}) async-start(), calls=%async_computation.7 | async-start | bytes 7864320 | tf_op jit(solution)/shard_map/reduce_scatter | solution.py:150
  373.3 12.6 %copy-start.8 = (bf16[512,6144]{1,0:T(8,128)(2,1)S(1)}, bf16[512,6144]{1,0:T(8,128)(2,1)}, u32[]{:S(2)}) copy-start(bf16[512,6144]{1,0:T(8,128)(2,1)} %all-gather.8.cloned.1.call-done) | copy-start | bytes 18874372
  373.3 24.4 %slice-start = ((s8[14155776]{0:T(1024)(128)(4,1)}), s8[4194304]{0:T(1024)(128)(4,1)S(1)}, s32[]{:S(2)}) async-start(s8[14155776]{0:T(1024)(128)(4,1)} %bitcast.110), calls=%async_computation.9 | async-start | bytes 8388608
  373.3 24.4 %slice-start.1 = ((s8[14155776]{0:T(1024)(128)(4,1)}), s8[4194304]{0:T(1024)(128)(4,1)S(1)}, s32[]{:S(2)}) async-start(s8[14155776]{0:T(1024)(128)(4,1)} %bitcast.110), calls=%async_computation.10 | async-start | bytes 8388608
  385.9 11.8 %slice-start.2 = ((s8[14155776]{0:T(1024)(128)(4,1)}), s8[4194304]{0:T(1024)(128)(4,1)S(1)}, s32[]{:S(2)}) async-start(s8[14155776]{0:T(1024)(128)(4,1)} %bitcast.110), calls=%async_computation.11 | async-start | bytes 8388608
  385.9 11.8 %slice-start.3 = ((s8[14155776]{0:T(1024)(128)(4,1)}), s8[1572864]{0:T(1024)(128)(4,1)S(1)}, s32[]{:S(2)}) async-start(s8[14155776]{0:T(1024)(128)(4,1)} %bitcast.110), calls=%async_computation.12 | async-start | bytes 3145728
  466.2 42.5 %all-to-all-start.1 = ((bf16[8,64,1536]{2,1,0:T(8,128)(2,1)}), bf16[8,64,1536]{2,1,0:T(8,128)(2,1)S(1)}, u32[]{:S(2)}, u32[]{:S(2)}) async-start(bf16[8,64,1536]{2,1,0:T(8,128)(2,1)} %bitcast.100), calls=%async_computation.3 | async-start | bytes 3145728 | tf_op jit(solution)/shard_map/all_to_all | solution.py:154
  510.0 3.2 copy-start.2
  510.0 4.0 copy-start.1
Sparse Core Ops, SparseCore 0:
  10.4 52.0 all-gather.9
  64.7 174.6 all-gather.5
  247.7 26.3 reduce-scatter.2
  328.9 44.4 all-gather.7
  407.8 58.3 reduce-scatter.4
where the time goes:
time: 521 us
  waiting for transfers between devices  357 us (69%)
  blocking collectives  71.4 us (14%)
  matrix products  44.2 us (8%)
  other arithmetic  18.3 us (4%)
  between operations  14.2 us (3%)
  local copies, waits for them, and re-layouts  9.65 us (2%)
  starting transfers between devices  5.86 us (1%)
    all_gather x1, waiting for transfers between devices, on_device(): lax.all_gather(out_weight, 'seq', axis=1, tiled=True)  166 us
    reduce_scatter x1, waiting for transfers between devices, on_device(): lax.psum_scatter(partial_value.astype(jnp.bfloat16), 'head', scatter_dime...  58.5 us
    all_gather x1, waiting for transfers between devices, on_device(): portion = lax.all_gather(flat_rows, 'head', axis=1, tiled=True)  44.3 us
    all_to_all x1, blocking collectives, on_device(): lax.all_to_all(outgoing, 'seq', split_axis=0, concat_axis=0, tiled=True)  42.4 us
    all_to_all x1, waiting for transfers between devices, on_device(): lax.all_to_all(returning, 'seq', split_axis=0, concat_axis=0, tiled=True)  36.5 us
    all_gather x1, waiting for transfers between devices, prefix(): lax.all_gather(part.astype(kind), axis)  26.4 us
    reduce_scatter x1, waiting for transfers between devices, on_device(): lax.psum_scatter(projected.astype(jnp.bfloat16), 'head', scatter_dimensio...  23.9 us
    unnamed x1, blocking collectives  23.2 us
  transfers between devices with their start and end apart: 6, of which 6 were waited for; matrix products, arithmetic and copies ran while one was open for 3% of the time, Pallas kernels for 0%

commit v1 on v0

--- a/solution.py
+++ b/solution.py
@@ -81,7 +81,8 @@
     query_heads = queries.reshape(shaped)
     key_heads = key_rows.reshape(shaped)
     value_heads = value_rows.reshape(shaped)
-    cumulative = jnp.cumsum(log_decay, axis=1)
+    upto = jnp.arange(tokens_here)[:, None] >= jnp.arange(tokens_here)[None, :]
+    cumulative = jnp.sum(jnp.where(upto[None], log_decay[:, None, :], 0.0), axis=-1)
     block_decay = cumulative[:, -1]
     local_state = block_state(key_heads, value_heads, cumulative)
     identity = (jnp.zeros_like(block_decay), jnp.zeros_like(local_state))
@@ -127,9 +128,11 @@
     chosen = jnp.sum(jnp.where(matches, logits[:, None, :], 0.0), axis=-1)
     gate_share = jax.nn.sigmoid(chosen - chosen[:, ::-1])
     capacity = 4 * tokens_here // experts
-    flat_hits = matches.reshape(tokens_here * 2, experts).astype(jnp.int32)
-    position = jnp.sum(jnp.cumsum(flat_hits, axis=0) * flat_hits, axis=1) - 1
-    slot_index = expert_ids.reshape(-1) * capacity + position
+    flat_ids = expert_ids.reshape(-1)
+    order = jnp.arange(tokens_here * 2)
+    ahead = (flat_ids[None, :] == flat_ids[:, None]) & (order[None, :] < order[:, None])
+    position = jnp.sum(ahead.astype(jnp.int32), axis=1)
+    slot_index = flat_ids * capacity + position
     target = slot_index[None, :] == jnp.arange(experts * capacity)[:, None]
     source = jnp.sum(jnp.where(target, jnp.arange(tokens_here * 2)[None, :] // 2, 0), axis=1)
     filled = jnp.any(target, axis=1)

time: 521 us -> 521 us (level)
  no operation moved by 1% of the time
where the time goes in v1:
time: 521 us
  waiting for transfers between devices  358 us (69%)
  blocking collectives  71.4 us (14%)
  matrix products  44.2 us (8%)
  other arithmetic  17.7 us (3%)
  between operations  14.2 us (3%)
  local copies, waits for them, and re-layouts  9.3 us (2%)
  starting transfers between devices  5.86 us (1%)
    all_gather x1, waiting for transfers between devices, on_device(): lax.all_gather(out_weight, 'seq', axis=1, tiled=True)  166 us
    reduce_scatter x1, waiting for transfers between devices, on_device(): lax.psum_scatter(partial_value.astype(jnp.bfloat16), 'head', scatter_dime...  58.5 us
    all_gather x1, waiting for transfers between devices, on_device(): portion = lax.all_gather(flat_rows, 'head', axis=1, tiled=True)  44.3 us
    all_to_all x1, blocking collectives, on_device(): lax.all_to_all(outgoing, 'seq', split_axis=0, concat_axis=0, tiled=True)  42.4 us
    all_to_all x1, waiting for transfers between devices, on_device(): lax.all_to_all(returning, 'seq', split_axis=0, concat_axis=0, tiled=True)  36.5 us
    all_gather x1, waiting for transfers between devices, prefix(): lax.all_gather(part.astype(kind), axis)  26.4 us
    reduce_scatter x1, waiting for transfers between devices, on_device(): lax.psum_scatter(projected.astype(jnp.bfloat16), 'head', scatter_dimensio...  24.8 us
    unnamed x1, blocking collectives  23.2 us
  transfers between devices with their start and end apart: 6, of which 6 were waited for; matrix products, arithmetic and copies ran while one was open for 3% of the time, Pallas kernels for 0%

profile of v1, /device:TPU:0, one launch (start us, length us, event | category | flops | bytes accessed | tf_op | source)
XLA Modules:
  0.0 520.5 jit_solution(4979863626688213314)
XLA Ops:
  7.7 1.1 copy.77
  12.8 23.2 %all-reduce = bf16[64]{0:T(256)(128)(2,1)S(1)} all-reduce(bf16[64]{0:T(256)(128)(2,1)S(1)} %dynamic-update-slice), channel_id=2, replica_groups=mesh['seq'=8,'head'=4] {'seq'}, use_global_device_ids=true, to_apply=%add | all-reduce | flops 64 | bytes 256
  36.0 26.4 %all-gather.10.cloned.1.call-done = bf16[64,128,128]{2,1,0:T(8,128)(2,1)} async-done(((bf16[8,128,128]{2,1,0:T(8,128)(2,1)}), bf16[64,128,128]{2,1,0:T(8,128)(2,1)}) %all-gather.10.cloned.1.call-update) | async-done | bytes 2097168 | tf_op jit(solution)/shard_map/all_gather | solution.py:17
  62.4 9.2 %while.16 = (s32[]{:T(128)}, f32[8]{0:T(128)S(1)}, f32[8,128,128]{2,1,0:T(8,128)S(1)}, s32[]{:T(128)}, bf16[8,8]{1,0:T(8,128)(2,1)S(1)}, /*index=5*/bf16[8,8,128,128]{3,2,1,0:T(8,128)(2,1)}, s32[]{:T(128)}, s32[]{:T(128)}) while((s32[]{:T(128)}, f32[8]{0:T(128)S(1)}, f32[8,128,128]{2,1,0:T(8,128)S(1)}, s32[]{:T(128)}, ...), condition=%wide.region_2.3_spmd.clone, body=%wide.region_1.2_spmd.clone.sunk | while | flops 655396 | bytes 1310979 | solution.py:30
  62.4 1.2 fusion.74
  63.6 1.1 fusion.74
  64.8 1.1 fusion.74
  65.9 1.1 fusion.74
  67.1 1.1 fusion.74
  68.2 1.1 fusion.74
  69.3 1.1 fusion.74
  70.5 1.1 fusion.74
  73.1 166.2 %all-gather.6.cloned.1.call-done = bf16[1024,6144]{1,0:T(8,128)(2,1)} async-done(((bf16[1024,768]{1,0:T(8,128)(2,1)}), bf16[1024,6144]{1,0:T(8,128)(2,1)}) %all-gather.6.cloned.1.call-update) | async-done | bytes 12582928 | tf_op jit(solution)/shard_map/all_gather | solution.py:100
  239.3 6.7 %fusion.62 = f32[128,6144]{1,0:T(8,128)S(1)} fusion(bf16[128,1024]{0,1:T(8,128)(2,1)S(1)} %bitcast.95, bf16[1024,6144]{1,0:T(8,128)(2,1)} %all-gather.6.cloned.1.call-done), kind=kOutput, calls=%fused_computation.93 | convolution fusion | flops 1610612736 | bytes 15990784 | tf_op jit(solution)/shard_map/dot_general | solution.py:98
  246.2 1.3 convert_element_type.95
  249.3 24.8 %reduce-scatter.3.cloned.1.call-done = bf16[128,1536]{1,0:T(8,128)(2,1)} async-done(((bf16[128,6144]{1,0:T(8,128)(2,1)}), bf16[128,1536]{1,0:T(8,128)(2,1)}) %reduce-scatter.3.cloned.1.call-update) | async-done | bytes 393232 | tf_op jit(solution)/shard_map/reduce_scatter | solution.py:110
  274.1 1.2 fusion.23
  275.2 1.7 fusion.21
  276.9 5.8 %all-reduce.1 = (f32[128]{0:T(128)S(1)}, f32[128,8]{0,1:T(8,128)S(1)}) all-reduce(f32[128]{0:T(128)S(1)} %fusion.23, f32[128,8]{0,1:T(8,128)S(1)} %fusion.21), channel_id=1, replica_groups=mesh['seq'=8,'head'=4] {'head'}, use_global_device_ids=true, to_apply=%region_7.8 | all-reduce | flops 1152 | bytes 9216 | tf_op jit(solution)/shard_map/psum | solution.py:116
  282.8 1.1 fusion.22
  283.9 2.1 gather_fusion
  286.2 42.4 %all_to_all.10 = bf16[8,64,1536]{2,1,0:T(8,128)(2,1)} all-to-all(bf16[8,64,1536]{2,1,0:T(8,128)(2,1)S(1)} %broadcast_select_fusion.2), channel_id=1, replica_groups=mesh['seq'=8,'head'=4] {'seq'}, dimensions={0} | all-to-all | bytes 3145728 | tf_op jit(solution)/shard_map/all_to_all | solution.py:145
  328.9 44.3 %all-gather.8.cloned.1.call-done = bf16[512,6144]{1,0:T(8,128)(2,1)} async-done(((bf16[512,1536]{1,0:T(8,128)(2,1)}), bf16[512,6144]{1,0:T(8,128)(2,1)}) %all-gather.8.cloned.1.call-update) | async-done | bytes 6291472 | tf_op jit(solution)/shard_map/all_gather | solution.py:148
  373.3 12.6 %fusion.5 = f32[512,1152]{1,0:T(8,128)S(1)} fusion(bf16[512,6144]{1,0:T(8,128)(2,1)} %all-gather.8.cloned.1.call-done, bf16[1,6144,1152]{2,1,0:T(8,128)(2,1)} %param.27), kind=kOutput, calls=%fused_computation.12 | convolution fusion | flops 7247757312 | bytes 22806528 | tf_op jit(solution)/shard_map/dot_general | solution.py:149
  385.9 11.7 %fusion.13 = bf16[512,1152]{1,0:T(8,128)(2,1)S(1)} fusion(bf16[512,6144]{1,0:T(8,128)(2,1)S(1)} %copy-done.8, bf16[1,6144,1152]{2,1,0:T(8,128)(2,1)} %param.28, f32[512,1152]{1,0:T(8,128)S(1)} %fusion.5), kind=kOutput, calls=%fused_computation.16 | convolution fusion | flops 7251296256 | bytes 23986176 | tf_op jit(solution)/shard_map/dot_general | solution.py:150
  397.7 10.0 %fusion.7 = bf16[512,6144]{1,0:T(8,128)(2,1)} fusion(bf16[512,1152]{1,0:T(8,128)(2,1)S(1)} %fusion.13, bf16[1,1152,6144]{2,1,0:T(8,128)(2,1)S(1)} %bitcast.105), kind=kOutput, calls=%fused_computation.14 | convolution fusion | flops 7250903040 | bytes 21626880 | tf_op jit(solution)/shard_map/dot_general | solution.py:152
  407.7 58.5 %reduce-scatter.5.cloned.1.call-done = bf16[512,1536]{1,0:T(8,128)(2,1)} async-done(((bf16[512,6144]{1,0:T(8,128)(2,1)}), bf16[512,1536]{1,0:T(8,128)(2,1)}) %reduce-scatter.5.cloned.1.call-update) | async-done | bytes 1572880 | tf_op jit(solution)/shard_map/reduce_scatter | solution.py:153
  466.2 5.5 %all-to-all-start.1 = ((bf16[8,64,1536]{2,1,0:T(8,128)(2,1)}), bf16[8,64,1536]{2,1,0:T(8,128)(2,1)S(1)}, u32[]{:S(2)}, u32[]{:S(2)}) async-start(bf16[8,64,1536]{2,1,0:T(8,128)(2,1)} %bitcast.94), calls=%async_computation.3 | async-start | bytes 3145728 | tf_op jit(solution)/shard_map/all_to_all | solution.py:157
  472.2 36.5 %all-to-all-done.1 = bf16[8,64,1536]{2,1,0:T(8,128)(2,1)S(1)} async-done(((bf16[8,64,1536]{2,1,0:T(8,128)(2,1)}), bf16[8,64,1536]{2,1,0:T(8,128)(2,1)S(1)}, u32[]{:S(2)}, u32[]{:S(2)}) %all-to-all-start.1) | async-done | bytes 1572896 | tf_op jit(solution)/shard_map/all_to_all | solution.py:157
  508.7 1.3 gather_fusion.1
  510.0 1.0 reshape.185
  511.0 2.2 multiply_reduce_fusion
  (89 shorter events, 9.5 us)
Async XLA Ops:
  6.5 2.4 copy-start
  6.5 4.5 copy-start.9
  6.5 55.9 %all-gather.10.cloned.1.call-start = ((), (), s32[]{:S(2)}) async-start(), calls=%async_computation.8 | async-start | bytes 2359296 | tf_op jit(solution)/shard_map/all_gather | solution.py:17
  10.2 229.2 %all-gather.6.cloned.1.call-start = ((), (), s32[]{:S(2)}) async-start(), calls=%async_computation.4 | async-start | bytes 14155776 | tf_op jit(solution)/shard_map/all_gather | solution.py:100
  10.9 263.1 %reduce-scatter.3.cloned.1.call-start = ((), (), s32[]{:S(2)}) async-start(), calls=%async_computation.5 | async-start | bytes 1966080 | tf_op jit(solution)/shard_map/reduce_scatter | solution.py:110
  62.4 9.3 %copy-start.3 = (f32[8,128,128]{2,1,0:T(8,128)S(1)}, f32[8,128,128]{2,1,0:T(8,128)}, u32[]{:S(2)}) copy-start(f32[8,128,128]{2,1,0:T(8,128)} %param.20) | copy-start | bytes 1572868
  62.4 9.3 %copy-start.5 = (bf16[128,1024]{1,0:T(8,128)(2,1)S(1)}, bf16[128,1024]{1,0:T(8,128)(2,1)}, u32[]{:S(2)}) copy-start(bf16[128,1024]{1,0:T(8,128)(2,1)} %param.16) | copy-start | bytes 786436
  71.7 1.2 copy-start.7
  239.3 6.7 %copy-start.4 = (bf16[128,1536]{1,0:T(8,128)(2,1)S(1)}, bf16[128,1536]{1,0:T(8,128)(2,1)}, u32[]{:S(2)}) copy-start(bf16[128,1536]{1,0:T(8,128)(2,1)} %param.23) | copy-start | bytes 1179652
  246.2 2.2 copy-start.6
  247.5 125.7 %all-gather.8.cloned.1.call-start = ((), (), s32[]{:S(2)}) async-start(), calls=%async_computation.6 | async-start | bytes 7864320 | tf_op jit(solution)/shard_map/all_gather | solution.py:148
  328.7 137.5 %reduce-scatter.5.cloned.1.call-start = ((), (), s32[]{:S(2)}) async-start(), calls=%async_computation.7 | async-start | bytes 7864320 | tf_op jit(solution)/shard_map/reduce_scatter | solution.py:153
  373.3 12.6 %copy-start.8 = (bf16[512,6144]{1,0:T(8,128)(2,1)S(1)}, bf16[512,6144]{1,0:T(8,128)(2,1)}, u32[]{:S(2)}) copy-start(bf16[512,6144]{1,0:T(8,128)(2,1)} %all-gather.8.cloned.1.call-done) | copy-start | bytes 18874372
  373.3 24.4 %slice-start = ((s8[14155776]{0:T(1024)(128)(4,1)}), s8[4194304]{0:T(1024)(128)(4,1)S(1)}, s32[]{:S(2)}) async-start(s8[14155776]{0:T(1024)(128)(4,1)} %bitcast.104), calls=%async_computation.9 | async-start | bytes 8388608
  373.3 24.4 %slice-start.1 = ((s8[14155776]{0:T(1024)(128)(4,1)}), s8[4194304]{0:T(1024)(128)(4,1)S(1)}, s32[]{:S(2)}) async-start(s8[14155776]{0:T(1024)(128)(4,1)} %bitcast.104), calls=%async_computation.10 | async-start | bytes 8388608
  385.9 11.8 %slice-start.2 = ((s8[14155776]{0:T(1024)(128)(4,1)}), s8[4194304]{0:T(1024)(128)(4,1)S(1)}, s32[]{:S(2)}) async-start(s8[14155776]{0:T(1024)(128)(4,1)} %bitcast.104), calls=%async_computation.11 | async-start | bytes 8388608
  385.9 11.8 %slice-start.3 = ((s8[14155776]{0:T(1024)(128)(4,1)}), s8[1572864]{0:T(1024)(128)(4,1)S(1)}, s32[]{:S(2)}) async-start(s8[14155776]{0:T(1024)(128)(4,1)} %bitcast.104), calls=%async_computation.12 | async-start | bytes 3145728
  466.2 42.5 %all-to-all-start.1 = ((bf16[8,64,1536]{2,1,0:T(8,128)(2,1)}), bf16[8,64,1536]{2,1,0:T(8,128)(2,1)S(1)}, u32[]{:S(2)}, u32[]{:S(2)}) async-start(bf16[8,64,1536]{2,1,0:T(8,128)(2,1)} %bitcast.94), calls=%async_computation.3 | async-start | bytes 3145728 | tf_op jit(solution)/shard_map/all_to_all | solution.py:157
  510.0 3.2 copy-start.2
  510.0 4.0 copy-start.1
Sparse Core Ops, SparseCore 0:
  10.3 52.0 all-gather.9
  64.6 174.6 all-gather.5
  247.7 26.3 reduce-scatter.2
  328.8 44.4 all-gather.7
  407.8 58.3 reduce-scatter.4

commit v2 on v1

--- a/solution.py
+++ b/solution.py
@@ -57,6 +57,35 @@
 
 def join_states(earlier, latter):
     return (earlier[0] + latter[0], jnp.exp(latter[0])[:, None, None] * earlier[1] + latter[1])
+
+
+def project(attn_rows, out_weight):
+    seq_size, head_size = (lax.axis_size("seq"), lax.axis_size("head"))
+    place = lax.axis_index("seq")
+    tokens_here = attn_rows.shape[0]
+    ratio = seq_size // head_size
+    all_rows = lax.all_gather(attn_rows, "seq", axis=0, tiled=True)
+    products = jnp.dot(all_rows, out_weight, preferred_element_type=jnp.float32)
+    sums = lax.psum_scatter(
+        products.astype(jnp.bfloat16), "head", scatter_dimension=0, tiled=True
+    ).reshape(ratio, tokens_here, -1)
+    landed = []
+    for turn in range(ratio):
+        pairs = [
+            (s * head_size + h, (ratio * h + (s + turn) % ratio) * head_size + s // ratio)
+            for s in range(seq_size)
+            for h in range(head_size)
+        ]
+        part = lax.dynamic_index_in_dim(sums, (place + turn) % ratio, 0, keepdims=False)
+        landed.append(lax.ppermute(part, ("seq", "head"), pairs))
+    landed = jnp.stack(landed)
+    return jnp.concatenate(
+        [
+            lax.dynamic_index_in_dim(landed, (place - b) % ratio, 0, keepdims=False)
+            for b in range(ratio)
+        ],
+        axis=1,
+    )
 
 
 def on_device(
@@ -95,21 +124,10 @@
         .reshape(tokens_here, heads_here * HEAD_DIM)
         .astype(jnp.bfloat16)
     )
-    projected = jnp.dot(
-        attn_rows,
-        lax.all_gather(out_weight, "seq", axis=1, tiled=True),
-        preferred_element_type=jnp.float32,
-    )
     width_here = residual.shape[1]
     first_column = lax.axis_index("head") * width_here
-    own_columns = lax.dynamic_slice_in_dim(
-        projected, first_column, width_here, 1
-    ) + residual.astype(jnp.float32)
-    projected = lax.dynamic_update_slice_in_dim(projected, own_columns, first_column, 1)
     experts = router.shape[1]
-    stream_here = lax.psum_scatter(
-        projected.astype(jnp.bfloat16), "head", scatter_dimension=1, tiled=True
-    ).astype(jnp.float32)
+    stream_here = residual.astype(jnp.float32) + project(attn_rows, out_weight).astype(jnp.float32)
     gain_here = lax.dynamic_slice_in_dim(ffn_gain, first_column, width_here, 0)
     router_here = lax.dynamic_slice_in_dim(router, first_column, width_here, 0)
     weighted = stream_here * gain_here

time: 521 us -> 430 us (0.83)
  waiting for transfers between devices: 358 us -> 245 us
  blocking collectives: 71.4 us -> 87 us
    all_gather x1, waiting for transfers between devices: 166 us -> 49.6 us  [project(): all_rows = lax.all_gather(attn_rows, 'seq', axis=0, tiled=True)]
    psum x1, blocking collectives: 5.85 us -> 22.2 us  [on_device(): lax.psum((jnp.sum(stream_here * stream_here, axis=-1), jnp.dot(weighted,...]
  transfers between devices with their start and end apart: 6 -> 8, of which waited for: 6 -> 7; matrix products, arithmetic and copies ran while one was open for 3% -> 1% of each run, Pallas kernels for 0% -> 0%
where the time goes in v2:
time: 430 us; the launch traced here: 429 us
  waiting for transfers between devices  245 us (57%)
  blocking collectives  87 us (20%)
  matrix products  45 us (10%)
  other arithmetic  16.1 us (4%)
  between operations  14.2 us (3%)
  local copies, waits for them, and re-layouts  13.9 us (3%)
  starting transfers between devices  8.08 us (2%)
    reduce_scatter x1, waiting for transfers between devices, on_device(): lax.psum_scatter(partial_value.astype(jnp.bfloat16), 'head', scatter_dime...  58.5 us
    all_gather x1, waiting for transfers between devices, project(): all_rows = lax.all_gather(attn_rows, 'seq', axis=0, tiled=True)  49.6 us
    all_gather x1, waiting for transfers between devices, on_device(): portion = lax.all_gather(flat_rows, 'head', axis=1, tiled=True)  44.8 us
    all_to_all x1, blocking collectives, on_device(): lax.all_to_all(outgoing, 'seq', split_axis=0, concat_axis=0, tiled=True)  41.6 us
    all_to_all x1, waiting for transfers between devices, on_device(): lax.all_to_all(returning, 'seq', split_axis=0, concat_axis=0, tiled=True)  35.9 us
    all_gather x1, waiting for transfers between devices, prefix(): lax.all_gather(part.astype(kind), axis)  26.9 us
    reduce_scatter x1, waiting for transfers between devices, project(): lax.psum_scatter(products.astype(jnp.bfloat16), 'head', scatter_dimension...  25.8 us
    unnamed x1, blocking collectives  23.2 us
  transfers between devices with their start and end apart: 8, of which 7 were waited for; matrix products, arithmetic and copies ran while one was open for 1% of the time, Pallas kernels for 0%

profile of v2, /device:TPU:0, one launch (start us, length us, event | category | flops | bytes accessed | tf_op | source)
XLA Modules:
  0.0 429.2 jit_solution(15826916656596974115)
XLA Ops:
  6.6 1.2 copy.77
  9.0 1.4 fusion.19
  11.3 1.2 dynamic-slice
  13.5 23.2 %all-reduce = bf16[64]{0:T(256)(128)(2,1)S(1)} all-reduce(bf16[64]{0:T(256)(128)(2,1)S(1)} %dynamic-update-slice), channel_id=2, replica_groups=mesh['seq'=8,'head'=4] {'seq'}, use_global_device_ids=true, to_apply=%add | all-reduce | flops 64 | bytes 256
  36.8 26.9 %all-gather.10.cloned.1.call-done = bf16[64,128,128]{2,1,0:T(8,128)(2,1)} async-done(((bf16[8,128,128]{2,1,0:T(8,128)(2,1)}), bf16[64,128,128]{2,1,0:T(8,128)(2,1)}) %all-gather.10.cloned.1.call-update) | async-done | bytes 2097168 | tf_op jit(solution)/shard_map/all_gather | solution.py:17
  63.7 9.1 %while.16 = (s32[]{:T(128)}, f32[8]{0:T(128)S(1)}, f32[8,128,128]{2,1,0:T(8,128)S(1)}, s32[]{:T(128)}, bf16[8,8]{1,0:T(8,128)(2,1)S(1)}, /*index=5*/bf16[8,8,128,128]{3,2,1,0:T(8,128)(2,1)}, s32[]{:T(128)}, s32[]{:T(128)}) while((s32[]{:T(128)}, f32[8]{0:T(128)S(1)}, f32[8,128,128]{2,1,0:T(8,128)S(1)}, s32[]{:T(128)}, ...), condition=%wide.region_2.3_spmd.clone, body=%wide.region_1.2_spmd.clone.sunk | while | flops 655396 | bytes 1310987 | solution.py:30
  63.7 1.1 fusion.74
  64.9 1.1 fusion.74
  67.2 1.1 fusion.74
  69.4 1.1 fusion.74
  70.6 1.1 fusion.74
  72.9 1.6 fusion.17
  74.5 1.5 multiply_reduce_fusion.2
  77.0 49.6 %all-gather.6.cloned.1.call-done = bf16[1024,1024]{0,1:T(8,128)(2,1)} async-done(((bf16[128,1024]{0,1:T(8,128)(2,1)}), bf16[1024,1024]{0,1:T(8,128)(2,1)}) %all-gather.6.cloned.1.call-update) | async-done | bytes 2097168 | tf_op jit(solution)/shard_map/all_gather | solution.py:67
  126.7 4.6 %convolution_convert_fusion = bf16[1024,768]{1,0:T(8,128)(2,1)} fusion(bf16[1024,1024]{0,1:T(8,128)(2,1)} %all-gather.6.cloned.1.call-done, bf16[1024,768]{1,0:T(8,128)(2,1)S(1)} %copy-done), kind=kOutput, calls=%fused_computation.17 | convolution fusion | flops 1611399168 | bytes 5242880 | tf_op jit(solution)/shard_map/dot_general | solution.py:68
  132.0 25.8 %reduce-scatter.3.cloned.1.call-done = bf16[256,768]{1,0:T(8,128)(2,1)} async-done(((bf16[1024,768]{1,0:T(8,128)(2,1)}), bf16[256,768]{1,0:T(8,128)(2,1)}) %reduce-scatter.3.cloned.1.call-update) | async-done | bytes 393232 | tf_op jit(solution)/shard_map/reduce_scatter | solution.py:69
  159.6 1.5 collective-permute-start.1
  162.2 3.1 collective-permute-done.1
  165.7 1.6 fusion.20
  167.3 22.2 %all-reduce.1 = (f32[128]{0:T(128)S(1)}, f32[128,8]{0,1:T(8,128)S(1)}) all-reduce(f32[128]{0:T(128)S(1)} %multiply_reduce_fusion.1, f32[128,8]{0,1:T(8,128)S(1)} %fusion.20), channel_id=1, replica_groups=mesh['seq'=8,'head'=4] {'head'}, use_global_device_ids=true, to_apply=%region_7.8 | all-reduce | flops 1152 | bytes 9216 | tf_op jit(solution)/shard_map/psum | solution.py:134
  189.7 2.1 gather_fusion
  192.0 41.6 %all_to_all.10 = bf16[8,64,1536]{2,1,0:T(8,128)(2,1)} all-to-all(bf16[8,64,1536]{2,1,0:T(8,128)(2,1)S(1)} %broadcast_select_fusion.2), channel_id=1, replica_groups=mesh['seq'=8,'head'=4] {'seq'}, dimensions={0} | all-to-all | bytes 3145728 | tf_op jit(solution)/shard_map/all_to_all | solution.py:163
  233.9 44.8 %all-gather.8.cloned.1.call-done = bf16[512,6144]{1,0:T(8,128)(2,1)} async-done(((bf16[512,1536]{1,0:T(8,128)(2,1)}), bf16[512,6144]{1,0:T(8,128)(2,1)}) %all-gather.8.cloned.1.call-update) | async-done | bytes 6291472 | tf_op jit(solution)/shard_map/all_gather | solution.py:166
  278.7 12.6 %fusion.5 = f32[512,1152]{1,0:T(8,128)S(1)} fusion(bf16[512,6144]{1,0:T(8,128)(2,1)} %all-gather.8.cloned.1.call-done, bf16[1,6144,1152]{2,1,0:T(8,128)(2,1)} %param.27), kind=kOutput, calls=%fused_computation.12 | convolution fusion | flops 7247757312 | bytes 22806528 | tf_op jit(solution)/shard_map/dot_general | solution.py:167
  291.3 11.7 %fusion.13 = bf16[512,1152]{1,0:T(8,128)(2,1)S(1)} fusion(bf16[512,6144]{1,0:T(8,128)(2,1)S(1)} %copy-done.10, bf16[1,6144,1152]{2,1,0:T(8,128)(2,1)} %param.28, f32[512,1152]{1,0:T(8,128)S(1)} %fusion.5), kind=kOutput, calls=%fused_computation.16 | convolution fusion | flops 7251296256 | bytes 23986176 | tf_op jit(solution)/shard_map/dot_general | solution.py:168
  303.1 10.1 %fusion.7 = bf16[512,6144]{1,0:T(8,128)(2,1)} fusion(bf16[512,1152]{1,0:T(8,128)(2,1)S(1)} %fusion.13, bf16[1,1152,6144]{2,1,0:T(8,128)(2,1)S(1)} %bitcast.119), kind=kOutput, calls=%fused_computation.14 | convolution fusion | flops 7250903040 | bytes 21626880 | tf_op jit(solution)/shard_map/dot_general | solution.py:170
  313.2 58.5 %reduce-scatter.5.cloned.1.call-done = bf16[512,1536]{1,0:T(8,128)(2,1)} async-done(((bf16[512,6144]{1,0:T(8,128)(2,1)}), bf16[512,1536]{1,0:T(8,128)(2,1)}) %reduce-scatter.5.cloned.1.call-update) | async-done | bytes 1572880 | tf_op jit(solution)/shard_map/reduce_scatter | solution.py:171
  371.7 5.5 %all-to-all-start.1 = ((bf16[8,64,1536]{2,1,0:T(8,128)(2,1)}), bf16[8,64,1536]{2,1,0:T(8,128)(2,1)S(1)}, u32[]{:S(2)}, u32[]{:S(2)}) async-start(bf16[8,64,1536]{2,1,0:T(8,128)(2,1)} %bitcast.105), calls=%async_computation.3 | async-start | bytes 3145728 | tf_op jit(solution)/shard_map/all_to_all | solution.py:175
  378.3 35.9 %all-to-all-done.1 = bf16[8,64,1536]{2,1,0:T(8,128)(2,1)S(1)} async-done(((bf16[8,64,1536]{2,1,0:T(8,128)(2,1)}), bf16[8,64,1536]{2,1,0:T(8,128)(2,1)S(1)}, u32[]{:S(2)}, u32[]{:S(2)}) %all-to-all-start.1) | async-done | bytes 1572896 | tf_op jit(solution)/shard_map/all_to_all | solution.py:175
  414.2 2.1 gather_fusion.1
  416.3 2.3 reshape.189
  418.7 3.2 multiply_reduce_fusion
  (95 shorter events, 13.4 us)
Async XLA Ops:
  6.5 120.2 %copy-start = (bf16[1024,768]{1,0:T(8,128)(2,1)S(1)}, bf16[1024,768]{1,0:T(8,128)(2,1)}, u32[]{:S(2)}) copy-start(bf16[1024,768]{1,0:T(8,128)(2,1)} %param.22) | copy-start | bytes 4718596
  6.5 57.1 %all-gather.10.cloned.1.call-start = ((), (), s32[]{:S(2)}) async-start(), calls=%async_computation.8 | async-start | bytes 2359296 | tf_op jit(solution)/shard_map/all_gather | solution.py:17
  11.2 115.5 %all-gather.6.cloned.1.call-start = ((), (), s32[]{:S(2)}) async-start(), calls=%async_computation.4 | async-start | bytes 2359296 | tf_op jit(solution)/shard_map/all_gather | solution.py:67
  63.7 9.2 %copy-start.7 = (f32[8,128,128]{2,1,0:T(8,128)S(1)}, f32[8,128,128]{2,1,0:T(8,128)}, u32[]{:S(2)}) copy-start(f32[8,128,128]{2,1,0:T(8,128)} %param.20) | copy-start | bytes 1572868
  72.8 3.2 copy-start.9
  77.0 54.4 %copy-start.8 = (s32[128,2]{0,1:T(2,128)S(1)}, s32[128,2]{0,1:T(2,128)}, u32[]{:S(2)}) copy-start(s32[128,2]{0,1:T(2,128)} %param.26) | copy-start | bytes 3076
  77.0 80.9 %reduce-scatter.3.cloned.1.call-start = ((), (), s32[]{:S(2)}) async-start(), calls=%async_computation.5 | async-start | bytes 1966080 | tf_op jit(solution)/shard_map/reduce_scatter | solution.py:69
  131.3 34.2 %copy-start.2 = (bf16[128,1536]{1,0:T(8,128)(2,1)S(1)}, bf16[128,1536]{1,0:T(8,128)(2,1)}, u32[]{:S(2)}) copy-start(bf16[128,1536]{1,0:T(8,128)(2,1)} %param.23) | copy-start | bytes 1179652
  131.3 147.4 %all-gather.8.cloned.1.call-start = ((), (), s32[]{:S(2)}) async-start(), calls=%async_computation.6 | async-start | bytes 7864320 | tf_op jit(solution)/shard_map/all_gather | solution.py:166
  158.9 3.3 collective-permute-start
  159.6 5.7 %collective-permute-start.1 = (bf16[128,768]{1,0:T(8,128)(2,1)S(1)}, bf16[128,768]{1,0:T(8,128)(2,1)S(1)}, u32[]{:S(2)}, u32[]{:S(2)}) collective-permute-start(bf16[128,768]{1,0:T(8,128)(2,1)S(1)} %get-tuple-element.168), channel_id=1, source_target_pairs={{0,4},{1,12},{2,20},{3,28},{4,0},{5,8},{6,16},{7,24},{8,5},{9,13},... | collective-permute-start | bytes 589832 | tf_op jit(solution)/shard_map/ppermute | solution.py:80
  165.5 24.0 %copy-start.3 = (bf16[128,768]{1,0:T(8,128)(2,1)}, bf16[128,768]{1,0:T(8,128)(2,1)S(1)}, u32[]{:S(2)}) copy-start(bf16[128,768]{1,0:T(8,128)(2,1)S(1)} %get-tuple-element.166) | copy-start | bytes 589828
  165.5 24.0 %copy-start.5 = (bf16[128,768]{1,0:T(8,128)(2,1)}, bf16[128,768]{1,0:T(8,128)(2,1)S(1)}, u32[]{:S(2)}) copy-start(bf16[128,768]{1,0:T(8,128)(2,1)S(1)} %get-tuple-element.167) | copy-start | bytes 589828
  233.7 138.0 %reduce-scatter.5.cloned.1.call-start = ((), (), s32[]{:S(2)}) async-start(), calls=%async_computation.7 | async-start | bytes 7864320 | tf_op jit(solution)/shard_map/reduce_scatter | solution.py:171
  278.7 12.6 %copy-start.10 = (bf16[512,6144]{1,0:T(8,128)(2,1)S(1)}, bf16[512,6144]{1,0:T(8,128)(2,1)}, u32[]{:S(2)}) copy-start(bf16[512,6144]{1,0:T(8,128)(2,1)} %all-gather.8.cloned.1.call-done) | copy-start | bytes 18874372
  278.7 24.4 %slice-start = ((s8[14155776]{0:T(1024)(128)(4,1)}), s8[4194304]{0:T(1024)(128)(4,1)S(1)}, s32[]{:S(2)}) async-start(s8[14155776]{0:T(1024)(128)(4,1)} %bitcast.118), calls=%async_computation.9 | async-start | bytes 8388608
  278.7 24.4 %slice-start.1 = ((s8[14155776]{0:T(1024)(128)(4,1)}), s8[4194304]{0:T(1024)(128)(4,1)S(1)}, s32[]{:S(2)}) async-start(s8[14155776]{0:T(1024)(128)(4,1)} %bitcast.118), calls=%async_computation.10 | async-start | bytes 8388608
  291.3 11.8 %slice-start.2 = ((s8[14155776]{0:T(1024)(128)(4,1)}), s8[4194304]{0:T(1024)(128)(4,1)S(1)}, s32[]{:S(2)}) async-start(s8[14155776]{0:T(1024)(128)(4,1)} %bitcast.118), calls=%async_computation.11 | async-start | bytes 8388608
  291.3 11.8 %slice-start.3 = ((s8[14155776]{0:T(1024)(128)(4,1)}), s8[1572864]{0:T(1024)(128)(4,1)S(1)}, s32[]{:S(2)}) async-start(s8[14155776]{0:T(1024)(128)(4,1)} %bitcast.118), calls=%async_computation.12 | async-start | bytes 3145728
  371.7 42.5 %all-to-all-start.1 = ((bf16[8,64,1536]{2,1,0:T(8,128)(2,1)}), bf16[8,64,1536]{2,1,0:T(8,128)(2,1)S(1)}, u32[]{:S(2)}, u32[]{:S(2)}) async-start(bf16[8,64,1536]{2,1,0:T(8,128)(2,1)} %bitcast.105), calls=%async_computation.3 | async-start | bytes 3145728 | tf_op jit(solution)/shard_map/all_to_all | solution.py:175
  416.3 6.4 %copy-start.1 = (bf16[1024,768]{1,0:T(8,128)(2,1)S(1)}, bf16[1024,768]{1,0:T(8,128)(2,1)}, u32[]{:S(2)}) copy-start(bf16[1024,768]{1,0:T(8,128)(2,1)} %param.22) | copy-start | bytes 4718596
  418.6 3.2 copy-start.4
  418.6 3.2 copy-start.6
Sparse Core Ops, SparseCore 0:
  11.3 52.3 all-gather.9
  77.1 49.5 all-gather.5
  131.4 26.3 reduce-scatter.2
  233.8 44.8 all-gather.7
  313.3 58.3 reduce-scatter.4

commit v3 on v2

--- a/solution.py
+++ b/solution.py
@@ -5,6 +5,7 @@
 
 D = 6144
 HEAD_DIM = 128
+CHUNKS = 2
 
 
 epsilon = 1e-06
@@ -160,19 +161,33 @@
     gate_here = gate_weight[0]
     up_here = up_weight[0]
     down_here = down_weight[0]
-    arrived = lax.all_to_all(outgoing, "seq", split_axis=0, concat_axis=0, tiled=True)
-    sources, slot_count, columns = arrived.shape
-    flat_rows = arrived.reshape(sources * slot_count, columns)
-    portion = lax.all_gather(flat_rows, "head", axis=1, tiled=True)
-    gate_act = jnp.dot(portion, gate_here, preferred_element_type=jnp.float32)
-    up_act = jnp.dot(portion, up_here, preferred_element_type=jnp.float32)
-    hidden = (jax.nn.silu(gate_act) * up_act).astype(jnp.bfloat16)
-    partial_value = jnp.dot(hidden, down_here, preferred_element_type=jnp.float32)
-    summed = lax.psum_scatter(
-        partial_value.astype(jnp.bfloat16), "head", scatter_dimension=1, tiled=True
-    )
-    returning = summed.reshape(sources, slot_count, -1)
-    returned = lax.all_to_all(returning, "seq", split_axis=0, concat_axis=0, tiled=True)
+    chunk = capacity // CHUNKS
+    arrivals = [
+        lax.all_to_all(
+            outgoing[:, c * chunk : (c + 1) * chunk],
+            "seq",
+            split_axis=0,
+            concat_axis=0,
+            tiled=True,
+        )
+        for c in range(CHUNKS)
+    ]
+    results = []
+    for arrived in arrivals:
+        flat_rows = arrived.reshape(experts * chunk, -1)
+        portion = lax.all_gather(flat_rows, "head", axis=1, tiled=True)
+        gate_act = jnp.dot(portion, gate_here, preferred_element_type=jnp.float32)
+        up_act = jnp.dot(portion, up_here, preferred_element_type=jnp.float32)
+        hidden = (jax.nn.silu(gate_act) * up_act).astype(jnp.bfloat16)
+        partial_value = jnp.dot(hidden, down_here, preferred_element_type=jnp.float32)
+        summed = lax.psum_scatter(
+            partial_value.astype(jnp.bfloat16), "head", scatter_dimension=1, tiled=True
+        )
+        returning = summed.reshape(experts, chunk, -1)
+        results.append(
+            lax.all_to_all(returning, "seq", split_axis=0, concat_axis=0, tiled=True)
+        )
+    returned = jnp.concatenate(results, axis=1)
     flat_back = returned.reshape(experts * capacity, -1)
     picked = flat_back[slot_index].reshape(tokens_here, 2, -1).astype(jnp.float32)
     mixture = jnp.sum(gate_share[:, :, None] * picked, axis=1)

time: 430 us -> 397 us (0.923)
  waiting for transfers between devices: 245 us -> 185 us
  matrix products: 45 us -> 60 us
  blocking collectives: 87 us -> 93.3 us
  starting transfers between devices: 8.08 us -> 13.7 us
    all_gather x1 -> x2, waiting for transfers between devices: 44.8 us -> 9.13 us  [on_device(): portion = lax.all_gather(flat_rows, 'head', axis=1, tiled=True)]
    all_to_all x1 -> x2, waiting for transfers between devices: 35.9 us -> 19.1 us  [on_device(): lax.all_to_all(returning, 'seq', split_axis=0, concat_axis=0, tiled=True)]
    dot_general x1 -> x2, matrix products: 12.6 us -> 21.6 us  [on_device(): gate_act = jnp.dot(portion, gate_here, preferred_element_type=jnp.float32)]
    reduce_scatter x1 -> x2, waiting for transfers between devices: 58.5 us -> 50.6 us  [on_device(): lax.psum_scatter(partial_value.astype(jnp.bfloat16), 'head', scatter_dime...]
    all_to_all x1 -> x2, blocking collectives: 41.6 us -> 47.9 us  [on_device(): lax.all_to_all(outgoing[:, c * chunk:(c + 1) * chunk], 'seq', split_axis=...]
    all_to_all x1 -> x2, starting transfers between devices: 5.52 us -> 11 us  [on_device(): lax.all_to_all(returning, 'seq', split_axis=0, concat_axis=0, tiled=True)]
    dot_general x1 -> x2, matrix products: 11.7 us -> 16.2 us  [on_device(): up_act = jnp.dot(portion, up_here, preferred_element_type=jnp.float32)]
    dot_general x1 -> x2, matrix products: 10.1 us -> 11.5 us  [on_device(): jnp.dot(hidden, down_here, preferred_element_type=jnp.float32)]
  transfers between devices with their start and end apart: 8 -> 11, of which waited for: 7 -> 9; matrix products, arithmetic and copies ran while one was open for 1% -> 13% of each run, Pallas kernels for 0% -> 0%
where the time goes in v3:
time: 397 us; the launch traced here: 396 us
  waiting for transfers between devices  185 us (47%)
  blocking collectives  93.3 us (24%)
  matrix products  60 us (15%)
  other arithmetic  16.4 us (4%)
  between operations  14.6 us (4%)
  starting transfers between devices  13.7 us (3%)
  local copies, waits for them, and re-layouts  13.2 us (3%)
    reduce_scatter x2, waiting for transfers between devices, on_device(): lax.psum_scatter(partial_value.astype(jnp.bfloat16), 'head', scatter_dime...  50.6 us
    all_gather x1, waiting for transfers between devices, project(): all_rows = lax.all_gather(attn_rows, 'seq', axis=0, tiled=True)  49.7 us
    all_to_all x2, blocking collectives, on_device(): lax.all_to_all(outgoing[:, c * chunk:(c + 1) * chunk], 'seq', split_axis=...  47.9 us
    all_gather x1, waiting for transfers between devices, prefix(): lax.all_gather(part.astype(kind), axis)  27.3 us
    reduce_scatter x1, waiting for transfers between devices, project(): lax.psum_scatter(products.astype(jnp.bfloat16), 'head', scatter_dimension...  25.8 us
    unnamed x1, blocking collectives  23.2 us
    psum x1, blocking collectives, on_device(): lax.psum((jnp.sum(stream_here * stream_here, axis=-1), jnp.dot(weighted,...  22.2 us
    dot_general x2, matrix products, on_device(): gate_act = jnp.dot(portion, gate_here, preferred_element_type=jnp.float32)  21.6 us
  transfers between devices with their start and end apart: 11, of which 9 were waited for; matrix products, arithmetic and copies ran while one was open for 13% of the time, Pallas kernels for 0%

profile of v3, /device:TPU:0, one launch (start us, length us, event | category | flops | bytes accessed | tf_op | source)
XLA Modules:
  0.0 396.2 jit_solution(14664821150121735816)
XLA Ops:
  9.0 1.4 fusion.34
  12.9 23.2 %all-reduce = bf16[64]{0:T(256)(128)(2,1)S(1)} all-reduce(bf16[64]{0:T(256)(128)(2,1)S(1)} %dynamic-update-slice), channel_id=2, replica_groups=mesh['seq'=8,'head'=4] {'seq'}, use_global_device_ids=true, to_apply=%add | all-reduce | flops 64 | bytes 256
  36.2 27.3 %all-gather.13.cloned.1.call-done = bf16[64,128,128]{2,1,0:T(8,128)(2,1)} async-done(((bf16[8,128,128]{2,1,0:T(8,128)(2,1)}), bf16[64,128,128]{2,1,0:T(8,128)(2,1)}) %all-gather.13.cloned.1.call-update) | async-done | bytes 2097168 | tf_op jit(solution)/shard_map/all_gather | solution.py:18
  63.5 9.1 %while.16 = (s32[]{:T(128)}, f32[8]{0:T(128)S(1)}, f32[8,128,128]{2,1,0:T(8,128)S(1)}, s32[]{:T(128)}, bf16[8,8]{1,0:T(8,128)(2,1)S(1)}, /*index=5*/bf16[8,8,128,128]{3,2,1,0:T(8,128)(2,1)}, s32[]{:T(128)}, s32[]{:T(128)}) while((s32[]{:T(128)}, f32[8]{0:T(128)S(1)}, f32[8,128,128]{2,1,0:T(8,128)S(1)}, s32[]{:T(128)}, ...), condition=%wide.region_2.3_spmd.clone, body=%wide.region_1.2_spmd.clone.sunk | while | flops 655396 | bytes 1310979 | solution.py:31
  72.7 1.6 fusion.32
  74.3 1.5 multiply_reduce_fusion.2
  76.9 49.7 %all-gather.7.cloned.1.call-done = bf16[1024,1024]{0,1:T(8,128)(2,1)} async-done(((bf16[128,1024]{0,1:T(8,128)(2,1)}), bf16[1024,1024]{0,1:T(8,128)(2,1)}) %all-gather.7.cloned.1.call-update) | async-done | bytes 2097168 | tf_op jit(solution)/shard_map/all_gather | solution.py:68
  126.5 4.6 %convolution_convert_fusion = bf16[1024,768]{1,0:T(8,128)(2,1)} fusion(bf16[1024,1024]{0,1:T(8,128)(2,1)} %all-gather.7.cloned.1.call-done, bf16[1024,768]{1,0:T(8,128)(2,1)S(1)} %copy-done), kind=kOutput, calls=%fused_computation.26 | convolution fusion | flops 1611399168 | bytes 5242880 | tf_op jit(solution)/shard_map/dot_general | solution.py:69
  131.9 25.8 %reduce-scatter.4.cloned.1.call-done = bf16[256,768]{1,0:T(8,128)(2,1)} async-done(((bf16[1024,768]{1,0:T(8,128)(2,1)}), bf16[256,768]{1,0:T(8,128)(2,1)}) %reduce-scatter.4.cloned.1.call-update) | async-done | bytes 393232 | tf_op jit(solution)/shard_map/reduce_scatter | solution.py:70
  159.3 1.6 collective-permute-start.1
  162.0 3.1 collective-permute-done.1
  165.5 1.6 fusion.35
  167.0 22.2 %all-reduce.1 = (f32[128]{0:T(128)S(1)}, f32[128,8]{0,1:T(8,128)S(1)}) all-reduce(f32[128]{0:T(128)S(1)} %multiply_reduce_fusion.1, f32[128,8]{0,1:T(8,128)S(1)} %fusion.35), channel_id=1, replica_groups=mesh['seq'=8,'head'=4] {'head'}, use_global_device_ids=true, to_apply=%region_7.8 | all-reduce | flops 1152 | bytes 9216 | tf_op jit(solution)/shard_map/psum | solution.py:135
  189.5 2.1 gather_fusion
  191.9 24.7 %all_to_all.20 = bf16[8,32,1536]{2,1,0:T(8,128)(2,1)} all-to-all(bf16[8,32,1536]{2,1,0:T(8,128)(2,1)S(1)} %get-tuple-element.166), channel_id=1, replica_groups=mesh['seq'=8,'head'=4] {'seq'}, dimensions={0} | all-to-all | bytes 1572864 | tf_op jit(solution)/shard_map/all_to_all | solution.py:166
  216.8 23.2 %all_to_all.21 = bf16[8,32,1536]{2,1,0:T(8,128)(2,1)} all-to-all(bf16[8,32,1536]{2,1,0:T(8,128)(2,1)S(1)} %get-tuple-element.167), channel_id=1, replica_groups=mesh['seq'=8,'head'=4] {'seq'}, dimensions={0} | all-to-all | bytes 1572864 | tf_op jit(solution)/shard_map/all_to_all | solution.py:166
  240.2 3.7 all-gather.9.cloned.1.call-done
  243.8 10.7 %fusion.11 = f32[256,1152]{1,0:T(8,128)S(1)} fusion(bf16[256,6144]{1,0:T(8,128)(2,1)} %all-gather.9.cloned.1.call-done, bf16[1,6144,1152]{2,1,0:T(8,128)(2,1)} %param.27), kind=kOutput, calls=%fused_computation.18 | convolution fusion | flops 3623878656 | bytes 18481152 | tf_op jit(solution)/shard_map/dot_general | solution.py:179
  254.6 8.0 %fusion.28 = bf16[256,1152]{1,0:T(8,128)(2,1)S(1)} fusion(bf16[256,6144]{1,0:T(8,128)(2,1)S(1)} %copy-done.11, bf16[1,6144,1152]{2,1,0:T(8,128)(2,1)} %param.28, f32[256,1152]{1,0:T(8,128)S(1)} %fusion.11), kind=kOutput, calls=%fused_computation.25 | convolution fusion | flops 3625648128 | bytes 19070976 | tf_op jit(solution)/shard_map/dot_general | solution.py:180
  262.6 5.7 %fusion.13 = bf16[256,6144]{1,0:T(8,128)(2,1)} fusion(bf16[256,1152]{1,0:T(8,128)(2,1)S(1)} %fusion.28, bf16[1,1152,6144]{2,1,0:T(8,128)(2,1)S(1)} %bitcast.138), kind=kOutput, calls=%fused_computation.20 | convolution fusion | flops 3625451520 | bytes 17891328 | tf_op jit(solution)/shard_map/dot_general | solution.py:182
  268.4 5.5 %all-gather.11.cloned.1.call-done = bf16[256,6144]{1,0:T(8,128)(2,1)} async-done(((bf16[256,1536]{1,0:T(8,128)(2,1)}), bf16[256,6144]{1,0:T(8,128)(2,1)}) %all-gather.11.cloned.1.call-update) | async-done | bytes 3145744 | tf_op jit(solution)/shard_map/all_gather | solution.py:178
  273.9 10.9 %fusion.9 = f32[256,1152]{1,0:T(8,128)S(1)} fusion(bf16[256,6144]{1,0:T(8,128)(2,1)} %all-gather.11.cloned.1.call-done, bf16[1,6144,1152]{2,1,0:T(8,128)(2,1)} %param.27), kind=kOutput, calls=%fused_computation.16 | convolution fusion | flops 3623878656 | bytes 18481152 | tf_op jit(solution)/shard_map/dot_general | solution.py:179
  284.8 8.3 %fusion.25 = bf16[256,1152]{1,0:T(8,128)(2,1)S(1)} fusion(bf16[256,6144]{1,0:T(8,128)(2,1)S(1)} %copy-done.10, bf16[1,6144,1152]{2,1,0:T(8,128)(2,1)} %param.28, f32[256,1152]{1,0:T(8,128)S(1)} %fusion.9), kind=kOutput, calls=%fused_computation.24 | convolution fusion | flops 3625648128 | bytes 19070976 | tf_op jit(solution)/shard_map/dot_general | solution.py:180
  293.1 5.7 %fusion.16 = bf16[256,6144]{1,0:T(8,128)(2,1)} fusion(bf16[256,1152]{1,0:T(8,128)(2,1)S(1)} %fusion.25, bf16[1,1152,6144]{2,1,0:T(8,128)(2,1)S(1)} %bitcast.140), kind=kOutput, calls=%fused_computation.21 | convolution fusion | flops 3625451520 | bytes 17891328 | tf_op jit(solution)/shard_map/dot_general | solution.py:182
  298.9 15.5 %reduce-scatter.6.cloned.1.call-done = bf16[256,1536]{1,0:T(8,128)(2,1)} async-done(((bf16[256,6144]{1,0:T(8,128)(2,1)}), bf16[256,1536]{1,0:T(8,128)(2,1)}) %reduce-scatter.6.cloned.1.call-update) | async-done | bytes 786448 | tf_op jit(solution)/shard_map/reduce_scatter | solution.py:183
  314.5 5.5 %all-to-all-start.1 = ((bf16[8,32,1536]{2,1,0:T(8,128)(2,1)}), bf16[8,32,1536]{2,1,0:T(8,128)(2,1)S(1)}, u32[]{:S(2)}, u32[]{:S(2)}) async-start(bf16[8,32,1536]{2,1,0:T(8,128)(2,1)} %bitcast.128), calls=%async_computation.3 | async-start | bytes 1572864 | tf_op jit(solution)/shard_map/all_to_all | solution.py:188
  320.0 35.0 %reduce-scatter.8.cloned.1.call-done = bf16[256,1536]{1,0:T(8,128)(2,1)} async-done(((bf16[256,6144]{1,0:T(8,128)(2,1)}), bf16[256,1536]{1,0:T(8,128)(2,1)}) %reduce-scatter.8.cloned.1.call-update) | async-done | bytes 786448 | tf_op jit(solution)/shard_map/reduce_scatter | solution.py:183
  355.0 5.5 %all-to-all-start.3 = ((bf16[8,32,1536]{2,1,0:T(8,128)(2,1)}), bf16[8,32,1536]{2,1,0:T(8,128)(2,1)S(1)}, u32[]{:S(2)}, u32[]{:S(2)}) async-start(bf16[8,32,1536]{2,1,0:T(8,128)(2,1)} %bitcast.127), calls=%async_computation.6 | async-start | bytes 1572864 | tf_op jit(solution)/shard_map/all_to_all | solution.py:188
  361.6 19.1 %all-to-all-done.3 = bf16[8,32,1536]{2,1,0:T(8,128)(2,1)S(1)} async-done(((bf16[8,32,1536]{2,1,0:T(8,128)(2,1)}), bf16[8,32,1536]{2,1,0:T(8,128)(2,1)S(1)}, u32[]{:S(2)}, u32[]{:S(2)}) %all-to-all-start.3) | async-done | bytes 786464 | tf_op jit(solution)/shard_map/all_to_all | solution.py:188
  380.8 2.1 gather_fusion.1
  383.0 2.3 reshape.197
  385.3 3.2 multiply_reduce_fusion
  (122 shorter events, 21.1 us)
Async XLA Ops:
  6.5 120.0 %copy-start = (bf16[1024,768]{1,0:T(8,128)(2,1)S(1)}, bf16[1024,768]{1,0:T(8,128)(2,1)}, u32[]{:S(2)}) copy-start(bf16[1024,768]{1,0:T(8,128)(2,1)} %param.22) | copy-start | bytes 4718596
  6.5 4.8 %copy-start.12 = (u32[32]{0:T(128)S(1)}, u32[32]{0:T(128)}, u32[]{:S(2)}) copy-start(u32[32]{0:T(128)} %constant.119) | copy-start | bytes 388
  6.5 56.9 %all-gather.13.cloned.1.call-start = ((), (), s32[]{:S(2)}) async-start(), calls=%async_computation.13 | async-start | bytes 2359296 | tf_op jit(solution)/shard_map/all_gather | solution.py:18
  11.2 115.3 %all-gather.7.cloned.1.call-start = ((), (), s32[]{:S(2)}) async-start(), calls=%async_computation.7 | async-start | bytes 2359296 | tf_op jit(solution)/shard_map/all_gather | solution.py:68
  63.5 9.2 %copy-start.7 = (f32[8,128,128]{2,1,0:T(8,128)S(1)}, f32[8,128,128]{2,1,0:T(8,128)}, u32[]{:S(2)}) copy-start(f32[8,128,128]{2,1,0:T(8,128)} %param.20) | copy-start | bytes 1572868
  72.6 3.2 copy-start.9
  76.8 54.4 %copy-start.8 = (s32[128,2]{0,1:T(2,128)S(1)}, s32[128,2]{0,1:T(2,128)}, u32[]{:S(2)}) copy-start(s32[128,2]{0,1:T(2,128)} %param.26) | copy-start | bytes 3076
  76.8 80.8 %reduce-scatter.4.cloned.1.call-start = ((), (), s32[]{:S(2)}) async-start(), calls=%async_computation.8 | async-start | bytes 1966080 | tf_op jit(solution)/shard_map/reduce_scatter | solution.py:70
  131.1 34.2 %copy-start.2 = (bf16[128,1536]{1,0:T(8,128)(2,1)S(1)}, bf16[128,1536]{1,0:T(8,128)(2,1)}, u32[]{:S(2)}) copy-start(bf16[128,1536]{1,0:T(8,128)(2,1)} %param.23) | copy-start | bytes 1179652
  131.1 112.7 %all-gather.9.cloned.1.call-start = ((), (), s32[]{:S(2)}) async-start(), calls=%async_computation.9 | async-start | bytes 3932160 | tf_op jit(solution)/shard_map/all_gather | solution.py:178
  158.7 3.3 collective-permute-start
  159.3 5.7 %collective-permute-start.1 = (bf16[128,768]{1,0:T(8,128)(2,1)S(1)}, bf16[128,768]{1,0:T(8,128)(2,1)S(1)}, u32[]{:S(2)}, u32[]{:S(2)}) collective-permute-start(bf16[128,768]{1,0:T(8,128)(2,1)S(1)} %get-tuple-element.170), channel_id=1, source_target_pairs={{0,4},{1,12},{2,20},{3,28},{4,0},{5,8},{6,16},{7,24},{8,5},{9,13},... | collective-permute-start | bytes 589832 | tf_op jit(solution)/shard_map/ppermute | solution.py:81
  165.2 24.1 %copy-start.3 = (bf16[128,768]{1,0:T(8,128)(2,1)}, bf16[128,768]{1,0:T(8,128)(2,1)S(1)}, u32[]{:S(2)}) copy-start(bf16[128,768]{1,0:T(8,128)(2,1)S(1)} %get-tuple-element.168) | copy-start | bytes 589828
  165.2 24.1 %copy-start.5 = (bf16[128,768]{1,0:T(8,128)(2,1)}, bf16[128,768]{1,0:T(8,128)(2,1)S(1)}, u32[]{:S(2)}) copy-start(bf16[128,768]{1,0:T(8,128)(2,1)S(1)} %get-tuple-element.169) | copy-start | bytes 589828
  216.7 57.2 %all-gather.11.cloned.1.call-start = ((), (), s32[]{:S(2)}) async-start(), calls=%async_computation.11 | async-start | bytes 3932160 | tf_op jit(solution)/shard_map/all_gather | solution.py:178
  239.9 74.5 %reduce-scatter.6.cloned.1.call-start = ((), (), s32[]{:S(2)}) async-start(), calls=%async_computation.10 | async-start | bytes 3932160 | tf_op jit(solution)/shard_map/reduce_scatter | solution.py:183
  243.8 10.7 %copy-start.11 = (bf16[256,6144]{1,0:T(8,128)(2,1)S(1)}, bf16[256,6144]{1,0:T(8,128)(2,1)}, u32[]{:S(2)}) copy-start(bf16[256,6144]{1,0:T(8,128)(2,1)} %all-gather.9.cloned.1.call-done) | copy-start | bytes 9437188
  243.8 18.7 %slice-start = ((s8[14155776]{0:T(1024)(128)(4,1)}), s8[4194304]{0:T(1024)(128)(4,1)S(1)}, s32[]{:S(2)}) async-start(s8[14155776]{0:T(1024)(128)(4,1)} %bitcast.137), calls=%async_computation.14 | async-start | bytes 8388608
  243.8 18.7 %slice-start.1 = ((s8[14155776]{0:T(1024)(128)(4,1)}), s8[4194304]{0:T(1024)(128)(4,1)S(1)}, s32[]{:S(2)}) async-start(s8[14155776]{0:T(1024)(128)(4,1)} %bitcast.137), calls=%async_computation.15 | async-start | bytes 8388608
  243.8 18.7 %slice-start.2 = ((s8[14155776]{0:T(1024)(128)(4,1)}), s8[4194304]{0:T(1024)(128)(4,1)S(1)}, s32[]{:S(2)}) async-start(s8[14155776]{0:T(1024)(128)(4,1)} %bitcast.137), calls=%async_computation.16 | async-start | bytes 8388608
  254.6 8.0 %slice-start.3 = ((s8[14155776]{0:T(1024)(128)(4,1)}), s8[1572864]{0:T(1024)(128)(4,1)S(1)}, s32[]{:S(2)}) async-start(s8[14155776]{0:T(1024)(128)(4,1)} %bitcast.137), calls=%async_computation.17 | async-start | bytes 3145728
  268.4 86.6 %reduce-scatter.8.cloned.1.call-start = ((), (), s32[]{:S(2)}) async-start(), calls=%async_computation.12 | async-start | bytes 3932160 | tf_op jit(solution)/shard_map/reduce_scatter | solution.py:183
  273.9 10.9 %copy-start.10 = (bf16[256,6144]{1,0:T(8,128)(2,1)S(1)}, bf16[256,6144]{1,0:T(8,128)(2,1)}, u32[]{:S(2)}) copy-start(bf16[256,6144]{1,0:T(8,128)(2,1)} %all-gather.11.cloned.1.call-done) | copy-start | bytes 9437188
  273.9 19.2 %slice-start.4 = ((s8[14155776]{0:T(1024)(128)(4,1)}), s8[4194304]{0:T(1024)(128)(4,1)S(1)}, s32[]{:S(2)}) async-start(s8[14155776]{0:T(1024)(128)(4,1)} %bitcast.139), calls=%async_computation.18 | async-start | bytes 8388608
  273.9 19.2 %slice-start.5 = ((s8[14155776]{0:T(1024)(128)(4,1)}), s8[4194304]{0:T(1024)(128)(4,1)S(1)}, s32[]{:S(2)}) async-start(s8[14155776]{0:T(1024)(128)(4,1)} %bitcast.139), calls=%async_computation.19 | async-start | bytes 8388608
  273.9 19.2 %slice-start.6 = ((s8[14155776]{0:T(1024)(128)(4,1)}), s8[4194304]{0:T(1024)(128)(4,1)S(1)}, s32[]{:S(2)}) async-start(s8[14155776]{0:T(1024)(128)(4,1)} %bitcast.139), calls=%async_computation.20 | async-start | bytes 8388608
  284.8 8.3 %slice-start.7 = ((s8[14155776]{0:T(1024)(128)(4,1)}), s8[1572864]{0:T(1024)(128)(4,1)S(1)}, s32[]{:S(2)}) async-start(s8[14155776]{0:T(1024)(128)(4,1)} %bitcast.139), calls=%async_computation.21 | async-start | bytes 3145728
  314.5 40.5 %all-to-all-start.1 = ((bf16[8,32,1536]{2,1,0:T(8,128)(2,1)}), bf16[8,32,1536]{2,1,0:T(8,128)(2,1)S(1)}, u32[]{:S(2)}, u32[]{:S(2)}) async-start(bf16[8,32,1536]{2,1,0:T(8,128)(2,1)} %bitcast.128), calls=%async_computation.3 | async-start | bytes 1572864 | tf_op jit(solution)/shard_map/all_to_all | solution.py:188
  355.0 25.7 %all-to-all-start.3 = ((bf16[8,32,1536]{2,1,0:T(8,128)(2,1)}), bf16[8,32,1536]{2,1,0:T(8,128)(2,1)S(1)}, u32[]{:S(2)}, u32[]{:S(2)}) async-start(bf16[8,32,1536]{2,1,0:T(8,128)(2,1)} %bitcast.127), calls=%async_computation.6 | async-start | bytes 1572864 | tf_op jit(solution)/shard_map/all_to_all | solution.py:188
  383.0 6.4 %copy-start.1 = (bf16[1024,768]{1,0:T(8,128)(2,1)S(1)}, bf16[1024,768]{1,0:T(8,128)(2,1)}, u32[]{:S(2)}) copy-start(bf16[1024,768]{1,0:T(8,128)(2,1)} %param.22) | copy-start | bytes 4718596
  385.3 3.2 copy-start.4
  385.3 3.2 copy-start.6
Sparse Core Ops, SparseCore 0:
  11.3 52.1 all-gather.12
  76.9 49.5 all-gather.6
  131.2 26.3 reduce-scatter.3
  216.8 26.9 all-gather.8
  245.3 28.5 all-gather.10
  276.4 37.9 reduce-scatter.5
  317.0 37.9 reduce-scatter.7

commit v4 on v3

--- a/solution.py
+++ b/solution.py
@@ -12,23 +12,31 @@
 highest = lax.Precision.HIGHEST
 
 
-def prefix(x, axis, combine, identity):
-    size, place = (lax.axis_size(axis), lax.axis_index(axis))
-    everything = jax.tree.map(
-        lambda part, kind: lax.all_gather(part.astype(kind), axis), x, (jnp.bfloat16, jnp.bfloat16)
-    )
-    start = jax.tree.map(
-        lambda part, zero: jnp.broadcast_to(jnp.asarray(zero, part.dtype), part.shape), x, identity
-    )
-
-    def turn(k, before):
-        reached = k < place
-        new = combine(
-            before, jax.tree.map(lambda part, own: part[k].astype(own.dtype), everything, x)
-        )
-        return jax.tree.map(lambda a, b: jnp.where(reached, a, b), new, before)
-
-    return lax.fori_loop(0, size, turn, start)
+def shift(x, turn, size, cyclic):
+    pairs = [(s, (s + turn) % size) for s in range(size) if cyclic or s + turn < size]
+    return lax.ppermute(x, "seq", pairs)
+
+
+def prior_blocks(block_decay, local_state):
+    size = lax.axis_size("seq")
+    heads, rows, width = local_state.shape
+    coarse = lax.reduce_precision(block_decay, 8, 7)
+    terms = jnp.concatenate([coarse, block_decay - coarse])
+    packed = jnp.concatenate(
+        [
+            local_state.reshape(heads * rows, width).astype(jnp.bfloat16),
+            jnp.broadcast_to(terms[:, None], (2 * heads, width)).astype(jnp.bfloat16),
+        ]
+    )
+    landed = [shift(packed, turn, size, False) for turn in range(1, size)]
+    decay = jnp.zeros_like(block_decay)
+    state = jnp.zeros_like(local_state)
+    for block in landed:
+        arrived = block[: heads * rows].astype(jnp.float32).reshape(heads, rows, width)
+        parts = block[heads * rows :, 0].astype(jnp.float32)
+        state = state + jnp.exp(decay)[:, None, None] * arrived
+        decay = decay + (parts[:heads] + parts[heads:])
+    return decay, state
 
 
 def block_attend(query_block, key_block, value_block, cumulative, entering):
@@ -56,33 +64,33 @@
     )
 
 
-def join_states(earlier, latter):
-    return (earlier[0] + latter[0], jnp.exp(latter[0])[:, None, None] * earlier[1] + latter[1])
-
-
 def project(attn_rows, out_weight):
     seq_size, head_size = (lax.axis_size("seq"), lax.axis_size("head"))
     place = lax.axis_index("seq")
     tokens_here = attn_rows.shape[0]
     ratio = seq_size // head_size
-    all_rows = lax.all_gather(attn_rows, "seq", axis=0, tiled=True)
-    products = jnp.dot(all_rows, out_weight, preferred_element_type=jnp.float32)
-    sums = lax.psum_scatter(
-        products.astype(jnp.bfloat16), "head", scatter_dimension=0, tiled=True
-    ).reshape(ratio, tokens_here, -1)
+    blocks = [attn_rows] + [shift(attn_rows, k, seq_size, True) for k in range(1, seq_size)]
+    products = jnp.concatenate(
+        [
+            jnp.dot(rows, out_weight, preferred_element_type=jnp.float32).astype(jnp.bfloat16)
+            for rows in blocks
+        ]
+    )
+    sums = lax.psum_scatter(products, "head", scatter_dimension=0, tiled=True).reshape(
+        ratio, tokens_here, -1
+    )
     landed = []
     for turn in range(ratio):
         pairs = [
-            (s * head_size + h, (ratio * h + (s + turn) % ratio) * head_size + s // ratio)
+            (s * head_size + h, (s - ratio * h - turn) % seq_size * head_size + s // ratio)
             for s in range(seq_size)
             for h in range(head_size)
         ]
-        part = lax.dynamic_index_in_dim(sums, (place + turn) % ratio, 0, keepdims=False)
-        landed.append(lax.ppermute(part, ("seq", "head"), pairs))
+        landed.append(lax.ppermute(sums[turn], ("seq", "head"), pairs))
     landed = jnp.stack(landed)
     return jnp.concatenate(
         [
-            lax.dynamic_index_in_dim(landed, (place - b) % ratio, 0, keepdims=False)
+            lax.dynamic_index_in_dim(landed, (b - place) % ratio, 0, keepdims=False)
             for b in range(ratio)
         ],
         axis=1,
@@ -115,8 +123,7 @@
     cumulative = jnp.sum(jnp.where(upto[None], log_decay[:, None, :], 0.0), axis=-1)
     block_decay = cumulative[:, -1]
     local_state = block_state(key_heads, value_heads, cumulative)
-    identity = (jnp.zeros_like(block_decay), jnp.zeros_like(local_state))
-    prior_decay, prior_state = prefix((block_decay, local_state), "seq", join_states, identity)
+    prior_decay, prior_state = prior_blocks(block_decay, local_state)
     entering = jnp.exp(prior_decay)[:, None, None] * init_state + prior_state
     attended = block_attend(query_heads, key_heads, value_heads, cumulative, entering)
     inverse = lax.rsqrt(jnp.mean(attended * attended, axis=-1, keepdims=True) + epsilon)

time: 397 us -> 408 us (1.028)
  starting transfers between devices: 13.7 us -> 77.1 us
  blocking collectives: 93.3 us -> 60.1 us
  waiting for transfers between devices: 185 us -> 157 us
  local copies, waits for them, and re-layouts: 13.2 us -> 20.8 us
    all_gather x2 -> x0, waiting for transfers between devices: 77 us -> none  [the longest x1 49.7 us: project(): all_rows = lax.all_gather(attn_rows, 'seq', axis=0, tiled=True)]
    ppermute x2 -> x16, starting transfers between devices: 2.23 us -> 65.7 us  [the longest x14 59.5 us: shift(): return lax.ppermute(x, 'seq', pairs)]
    ppermute x2 -> x16, waiting for transfers between devices: 3.13 us -> 35.1 us  [the longest x14 30.8 us: shift(): return lax.ppermute(x, 'seq', pairs)]
    unnamed x1 -> x0, blocking collectives: 23.2 us -> none
    reduce_scatter x1, waiting for transfers between devices: 25.8 us -> 42.7 us  [project(): lax.psum_scatter(products, 'head', scatter_dimension=0, tiled=True)]
    reshape x0 -> x7, other arithmetic: none -> 10 us  [prior_blocks(): block[:heads * rows].astype(jnp.float32).reshape(heads, rows, width)]
    psum x1, blocking collectives: 22.2 us -> 12.2 us  [on_device(): lax.psum((jnp.sum(stream_here * stream_here, axis=-1), jnp.dot(weighted,...]
    reshape x1 -> x8, local copies, waits for them, and re-layouts: 1.14 us -> 10.9 us  [the longest x7 9.77 us: prior_blocks(): block[:heads * rows].astype(jnp.float32).reshape(heads, rows, width)]
  transfers between devices with their start and end apart: 11 -> 23, of which waited for: 9 -> 13; matrix products, arithmetic and copies ran while one was open for 13% -> 13% of each run, Pallas kernels for 0% -> 0%
where the time goes in v4:
time: 408 us; the launch traced here: 406 us
  waiting for transfers between devices  157 us (38%)
  starting transfers between devices  77.1 us (19%)
  matrix products  60.5 us (15%)
  blocking collectives  60.1 us (15%)
  local copies, waits for them, and re-layouts  20.8 us (5%)
  other arithmetic  17.1 us (4%)
  between operations  14 us (3%)
    ppermute x14, starting transfers between devices, shift(): return lax.ppermute(x, 'seq', pairs)  59.5 us
    reduce_scatter x2, waiting for transfers between devices, on_device(): lax.psum_scatter(partial_value.astype(jnp.bfloat16), 'head', scatter_dime...  50.4 us
    all_to_all x2, blocking collectives, on_device(): lax.all_to_all(outgoing[:, c * chunk:(c + 1) * chunk], 'seq', split_axis=...  47.9 us
    reduce_scatter x1, waiting for transfers between devices, project(): lax.psum_scatter(products, 'head', scatter_dimension=0, tiled=True)  42.7 us
    ppermute x14, waiting for transfers between devices, shift(): return lax.ppermute(x, 'seq', pairs)  30.8 us
    dot_general x2, matrix products, on_device(): gate_act = jnp.dot(portion, gate_here, preferred_element_type=jnp.float32)  21.4 us
    all_to_all x2, waiting for transfers between devices, on_device(): lax.all_to_all(returning, 'seq', split_axis=0, concat_axis=0, tiled=True)  19.1 us
    dot_general x2, matrix products, on_device(): up_act = jnp.dot(portion, up_here, preferred_element_type=jnp.float32)  16.2 us
  transfers between devices with their start and end apart: 23, of which 13 were waited for; matrix products, arithmetic and copies ran while one was open for 13% of the time, Pallas kernels for 0%

profile of v4, /device:TPU:0, one launch (start us, length us, event | category | flops | bytes accessed | tf_op | source)
XLA Modules:
  0.0 406.4 jit_solution(15355872241958370742)
XLA Ops:
  10.8 5.9 %collective-permute-start.3 = (bf16[1040,128]{0,1:T(8,128)(2,1)S(1)}, bf16[1040,128]{0,1:T(8,128)(2,1)S(1)}, u32[]{:S(2)}, u32[]{:S(2)}) collective-permute-start(bf16[1040,128]{0,1:T(8,128)(2,1)S(1)} %pad_maximum_fusion.2), channel_id=1, source_target_pairs={{0,16},{4,20},{8,24},{12,28},{1,17},{5,21},{9,25},{13,29},{2,18},{... | collective-permute-start | bytes 798728 | tf_op jit(solution)/shard_map/ppermute | solution.py:17
  16.7 4.5 %collective-permute-start.2 = (bf16[1040,128]{0,1:T(8,128)(2,1)S(1)}, bf16[1040,128]{0,1:T(8,128)(2,1)S(1)}, u32[]{:S(2)}, u32[]{:S(2)}) collective-permute-start(bf16[1040,128]{0,1:T(8,128)(2,1)S(1)} %pad_maximum_fusion.2), channel_id=1, source_target_pairs={{0,12},{4,16},{8,20},{12,24},{16,28},{1,13},{5,17},{9,21},{13,25},... | collective-permute-start | bytes 798728 | tf_op jit(solution)/shard_map/ppermute | solution.py:17
  22.5 3.1 collective-permute-start
  27.0 8.7 %collective-permute-start.5 = (bf16[1040,128]{0,1:T(8,128)(2,1)S(1)}, bf16[1040,128]{0,1:T(8,128)(2,1)S(1)}, u32[]{:S(2)}, u32[]{:S(2)}) collective-permute-start(bf16[1040,128]{0,1:T(8,128)(2,1)S(1)} %pad_maximum_fusion.2), channel_id=1, source_target_pairs={{0,24},{4,28},{1,25},{5,29},{2,26},{6,30},{3,27},{7,31}} | collective-permute-start | bytes 798728 | tf_op jit(solution)/shard_map/ppermute | solution.py:17
  35.6 7.5 %collective-permute-start.4 = (bf16[1040,128]{0,1:T(8,128)(2,1)S(1)}, bf16[1040,128]{0,1:T(8,128)(2,1)S(1)}, u32[]{:S(2)}, u32[]{:S(2)}) collective-permute-start(bf16[1040,128]{0,1:T(8,128)(2,1)S(1)} %pad_maximum_fusion.2), channel_id=1, source_target_pairs={{0,20},{4,24},{8,28},{1,21},{5,25},{9,29},{2,22},{6,26},{10,30},{3... | collective-permute-start | bytes 798728 | tf_op jit(solution)/shard_map/ppermute | solution.py:17
  43.2 6.3 %collective-permute-done.5 = bf16[1040,128]{0,1:T(8,128)(2,1)S(1)} collective-permute-done((bf16[1040,128]{0,1:T(8,128)(2,1)S(1)}, bf16[1040,128]{0,1:T(8,128)(2,1)S(1)}, u32[]{:S(2)}, u32[]{:S(2)}) %collective-permute-start.5) | collective-permute-done | bytes 266272 | tf_op jit(solution)/shard_map/ppermute | solution.py:17
  49.5 5.2 %collective-permute-done.4 = bf16[1040,128]{0,1:T(8,128)(2,1)S(1)} collective-permute-done((bf16[1040,128]{0,1:T(8,128)(2,1)S(1)}, bf16[1040,128]{0,1:T(8,128)(2,1)S(1)}, u32[]{:S(2)}, u32[]{:S(2)}) %collective-permute-start.4) | collective-permute-done | bytes 266272 | tf_op jit(solution)/shard_map/ppermute | solution.py:17
  75.3 3.4 fusion.31
  83.0 13.5 %collective-permute-start.8 = (bf16[128,1024]{0,1:T(8,128)(2,1)S(1)}, bf16[128,1024]{0,1:T(8,128)(2,1)S(1)}, u32[]{:S(2)}, u32[]{:S(2)}) collective-permute-start(bf16[128,1024]{0,1:T(8,128)(2,1)S(1)} %bitcast.153), channel_id=1, source_target_pairs={{0,8},{4,12},{8,16},{12,20},{16,24},{20,28},{24,0},{28,4},{1,9},{5... | collective-permute-start | bytes 786440 | tf_op jit(solution)/shard_map/ppermute | solution.py:17
  100.0 3.4 collective-permute-start.11
  106.2 4.5 %collective-permute-start.13 = (bf16[128,1024]{0,1:T(8,128)(2,1)S(1)}, bf16[128,1024]{0,1:T(8,128)(2,1)S(1)}, u32[]{:S(2)}, u32[]{:S(2)}) collective-permute-start(bf16[128,1024]{0,1:T(8,128)(2,1)S(1)} %bitcast.159), channel_id=1, source_target_pairs={{0,28},{4,0},{8,4},{12,8},{16,12},{20,16},{24,20},{28,24},{1,29},{... | collective-permute-start | bytes 786440 | tf_op jit(solution)/shard_map/ppermute | solution.py:17
  111.2 16.3 %collective-permute-done.9 = bf16[128,1024]{0,1:T(8,128)(2,1)S(1)} collective-permute-done((bf16[128,1024]{0,1:T(8,128)(2,1)S(1)}, bf16[128,1024]{0,1:T(8,128)(2,1)S(1)}, u32[]{:S(2)}, u32[]{:S(2)}) %collective-permute-start.9) | collective-permute-done | bytes 262176 | tf_op jit(solution)/shard_map/ppermute | solution.py:17
  132.4 42.7 %reduce-scatter.4.cloned.1.call-done = bf16[256,768]{1,0:T(8,128)(2,1)} async-done(((bf16[1024,768]{1,0:T(8,128)(2,1)}), bf16[256,768]{1,0:T(8,128)(2,1)}) %reduce-scatter.4.cloned.1.call-update) | async-done | bytes 393232 | tf_op jit(solution)/shard_map/reduce_scatter | solution.py:79
  176.9 5.6 %collective-permute-start.15 = (bf16[128,768]{1,0:T(8,128)(2,1)S(1)}, bf16[128,768]{1,0:T(8,128)(2,1)S(1)}, u32[]{:S(2)}, u32[]{:S(2)}) collective-permute-start(bf16[128,768]{1,0:T(8,128)(2,1)S(1)} %get-tuple-element.17), channel_id=1, source_target_pairs={{0,28},{1,20},{2,12},{3,4},{4,0},{5,24},{6,16},{7,8},{8,5},{9,29},... | collective-permute-start | bytes 589832 | tf_op jit(solution)/shard_map/ppermute | solution.py:89
  183.5 4.3 %collective-permute-done.15 = bf16[128,768]{1,0:T(8,128)(2,1)S(1)} collective-permute-done((bf16[128,768]{1,0:T(8,128)(2,1)S(1)}, bf16[128,768]{1,0:T(8,128)(2,1)S(1)}, u32[]{:S(2)}, u32[]{:S(2)}) %collective-permute-start.15) | collective-permute-done | bytes 196640 | tf_op jit(solution)/shard_map/ppermute | solution.py:89
  189.7 12.2 %all-reduce = (f32[128]{0:T(128)S(1)}, f32[128,8]{0,1:T(8,128)S(1)}) all-reduce(f32[128]{0:T(128)S(1)} %multiply_reduce_fusion.1, f32[128,8]{0,1:T(8,128)S(1)} %fusion.41), channel_id=1, replica_groups=mesh['seq'=8,'head'=4] {'head'}, use_global_device_ids=true, to_apply=%region_5.6 | all-reduce | flops 1152 | bytes 9216 | tf_op jit(solution)/shard_map/psum | solution.py:142
  204.6 24.8 %all_to_all.20 = bf16[8,32,1536]{2,1,0:T(8,128)(2,1)} all-to-all(bf16[8,32,1536]{2,1,0:T(8,128)(2,1)S(1)} %get-tuple-element.13), channel_id=1, replica_groups=mesh['seq'=8,'head'=4] {'seq'}, dimensions={0} | all-to-all | bytes 1572864 | tf_op jit(solution)/shard_map/all_to_all | solution.py:173
  229.5 23.2 %all_to_all.21 = bf16[8,32,1536]{2,1,0:T(8,128)(2,1)} all-to-all(bf16[8,32,1536]{2,1,0:T(8,128)(2,1)S(1)} %get-tuple-element.14), channel_id=1, replica_groups=mesh['seq'=8,'head'=4] {'seq'}, dimensions={0} | all-to-all | bytes 1572864 | tf_op jit(solution)/shard_map/all_to_all | solution.py:173
  252.9 3.6 all-gather.3.cloned.1.call-done
  256.5 10.6 %fusion.10 = f32[256,1152]{1,0:T(8,128)S(1)} fusion(bf16[256,6144]{1,0:T(8,128)(2,1)} %all-gather.3.cloned.1.call-done, bf16[1,6144,1152]{2,1,0:T(8,128)(2,1)} %param.25), kind=kOutput, calls=%fused_computation.12 | convolution fusion | flops 3623878656 | bytes 18481152 | tf_op jit(solution)/shard_map/dot_general | solution.py:186
  267.1 8.0 %fusion.27 = bf16[256,1152]{1,0:T(8,128)(2,1)S(1)} fusion(bf16[256,6144]{1,0:T(8,128)(2,1)S(1)} %copy-done.17, bf16[1,6144,1152]{2,1,0:T(8,128)(2,1)} %param.26, f32[256,1152]{1,0:T(8,128)S(1)} %fusion.10), kind=kOutput, calls=%fused_computation.19 | convolution fusion | flops 3625648128 | bytes 19070976 | tf_op jit(solution)/shard_map/dot_general | solution.py:187
  275.2 5.7 %fusion.12 = bf16[256,6144]{1,0:T(8,128)(2,1)} fusion(bf16[256,1152]{1,0:T(8,128)(2,1)S(1)} %fusion.27, bf16[1,1152,6144]{2,1,0:T(8,128)(2,1)S(1)} %bitcast.170), kind=kOutput, calls=%fused_computation.14 | convolution fusion | flops 3625451520 | bytes 17891328 | tf_op jit(solution)/shard_map/dot_general | solution.py:189
  281.0 5.8 %all-gather.5.cloned.1.call-done = bf16[256,6144]{1,0:T(8,128)(2,1)} async-done(((bf16[256,1536]{1,0:T(8,128)(2,1)}), bf16[256,6144]{1,0:T(8,128)(2,1)}) %all-gather.5.cloned.1.call-update) | async-done | bytes 3145744 | tf_op jit(solution)/shard_map/all_gather | solution.py:185
  286.7 10.8 %fusion.8 = f32[256,1152]{1,0:T(8,128)S(1)} fusion(bf16[256,6144]{1,0:T(8,128)(2,1)} %all-gather.5.cloned.1.call-done, bf16[1,6144,1152]{2,1,0:T(8,128)(2,1)} %param.25), kind=kOutput, calls=%fused_computation.10 | convolution fusion | flops 3623878656 | bytes 18481152 | tf_op jit(solution)/shard_map/dot_general | solution.py:186
  297.6 8.3 %fusion.24 = bf16[256,1152]{1,0:T(8,128)(2,1)S(1)} fusion(bf16[256,6144]{1,0:T(8,128)(2,1)S(1)} %copy-done.16, bf16[1,6144,1152]{2,1,0:T(8,128)(2,1)} %param.26, f32[256,1152]{1,0:T(8,128)S(1)} %fusion.8), kind=kOutput, calls=%fused_computation.18 | convolution fusion | flops 3625648128 | bytes 19070976 | tf_op jit(solution)/shard_map/dot_general | solution.py:187
  305.9 5.7 %fusion.15 = bf16[256,6144]{1,0:T(8,128)(2,1)} fusion(bf16[256,1152]{1,0:T(8,128)(2,1)S(1)} %fusion.24, bf16[1,1152,6144]{2,1,0:T(8,128)(2,1)S(1)} %bitcast.172), kind=kOutput, calls=%fused_computation.15 | convolution fusion | flops 3625451520 | bytes 17891328 | tf_op jit(solution)/shard_map/dot_general | solution.py:189
  311.7 15.6 %reduce-scatter.6.cloned.1.call-done = bf16[256,1536]{1,0:T(8,128)(2,1)} async-done(((bf16[256,6144]{1,0:T(8,128)(2,1)}), bf16[256,1536]{1,0:T(8,128)(2,1)}) %reduce-scatter.6.cloned.1.call-update) | async-done | bytes 786448 | tf_op jit(solution)/shard_map/reduce_scatter | solution.py:190
  327.3 5.5 %all-to-all-start.1 = ((bf16[8,32,1536]{2,1,0:T(8,128)(2,1)}), bf16[8,32,1536]{2,1,0:T(8,128)(2,1)S(1)}, u32[]{:S(2)}, u32[]{:S(2)}) async-start(bf16[8,32,1536]{2,1,0:T(8,128)(2,1)} %bitcast.161), calls=%async_computation.3 | async-start | bytes 1572864 | tf_op jit(solution)/shard_map/all_to_all | solution.py:195
  332.8 34.8 %reduce-scatter.8.cloned.1.call-done = bf16[256,1536]{1,0:T(8,128)(2,1)} async-done(((bf16[256,6144]{1,0:T(8,128)(2,1)}), bf16[256,1536]{1,0:T(8,128)(2,1)}) %reduce-scatter.8.cloned.1.call-update) | async-done | bytes 786448 | tf_op jit(solution)/shard_map/reduce_scatter | solution.py:190
  367.6 5.5 %all-to-all-start.3 = ((bf16[8,32,1536]{2,1,0:T(8,128)(2,1)}), bf16[8,32,1536]{2,1,0:T(8,128)(2,1)S(1)}, u32[]{:S(2)}, u32[]{:S(2)}) async-start(bf16[8,32,1536]{2,1,0:T(8,128)(2,1)} %bitcast.160), calls=%async_computation.6 | async-start | bytes 1572864 | tf_op jit(solution)/shard_map/all_to_all | solution.py:195
  374.3 19.1 %all-to-all-done.3 = bf16[8,32,1536]{2,1,0:T(8,128)(2,1)S(1)} async-done(((bf16[8,32,1536]{2,1,0:T(8,128)(2,1)}), bf16[8,32,1536]{2,1,0:T(8,128)(2,1)S(1)}, u32[]{:S(2)}, u32[]{:S(2)}) %all-to-all-start.3) | async-done | bytes 786464 | tf_op jit(solution)/shard_map/all_to_all | solution.py:195
  395.8 3.2 multiply_reduce_fusion
  (163 shorter events, 55.3 us)
Async XLA Ops:
  6.5 96.8 %copy-start = (bf16[1024,768]{1,0:T(8,128)(2,1)S(1)}, bf16[1024,768]{1,0:T(8,128)(2,1)}, u32[]{:S(2)}) copy-start(bf16[1024,768]{1,0:T(8,128)(2,1)} %param.20) | copy-start | bytes 4718596
  6.5 168.6 %reduce-scatter.4.cloned.1.call-start = ((), (), s32[]{:S(2)}) async-start(), calls=%async_computation.7 | async-start | bytes 1966080 | tf_op jit(solution)/shard_map/reduce_scatter | solution.py:79
  10.8 16.2 %collective-permute-start.3 = (bf16[1040,128]{0,1:T(8,128)(2,1)S(1)}, bf16[1040,128]{0,1:T(8,128)(2,1)S(1)}, u32[]{:S(2)}, u32[]{:S(2)}) collective-permute-start(bf16[1040,128]{0,1:T(8,128)(2,1)S(1)} %pad_maximum_fusion.2), channel_id=1, source_target_pairs={{0,16},{4,20},{8,24},{12,28},{1,17},{5,21},{9,25},{13,29},{2,18},{... | collective-permute-start | bytes 798728 | tf_op jit(solution)/shard_map/ppermute | solution.py:17
  16.7 18.9 %collective-permute-start.2 = (bf16[1040,128]{0,1:T(8,128)(2,1)S(1)}, bf16[1040,128]{0,1:T(8,128)(2,1)S(1)}, u32[]{:S(2)}, u32[]{:S(2)}) collective-permute-start(bf16[1040,128]{0,1:T(8,128)(2,1)S(1)} %pad_maximum_fusion.2), channel_id=1, source_target_pairs={{0,12},{4,16},{8,20},{12,24},{16,28},{1,13},{5,17},{9,21},{13,25},... | collective-permute-start | bytes 798728 | tf_op jit(solution)/shard_map/ppermute | solution.py:17
  21.2 21.9 %collective-permute-start.1 = (bf16[1040,128]{0,1:T(8,128)(2,1)S(1)}, bf16[1040,128]{0,1:T(8,128)(2,1)S(1)}, u32[]{:S(2)}, u32[]{:S(2)}) collective-permute-start(bf16[1040,128]{0,1:T(8,128)(2,1)S(1)} %pad_maximum_fusion.2), channel_id=1, source_target_pairs={{0,8},{4,12},{8,16},{12,20},{16,24},{20,28},{1,9},{5,13},{9,17},{1... | collective-permute-start | bytes 798728 | tf_op jit(solution)/shard_map/ppermute | solution.py:17
  22.5 20.6 %collective-permute-start = (bf16[1040,128]{0,1:T(8,128)(2,1)S(1)}, bf16[1040,128]{0,1:T(8,128)(2,1)S(1)}, u32[]{:S(2)}, u32[]{:S(2)}) collective-permute-start(bf16[1040,128]{0,1:T(8,128)(2,1)S(1)} %pad_maximum_fusion.2), channel_id=1, source_target_pairs={{0,4},{4,8},{8,12},{12,16},{16,20},{20,24},{24,28},{1,5},{5,9},{9,... | collective-permute-start | bytes 798728 | tf_op jit(solution)/shard_map/ppermute | solution.py:17
  25.6 17.6 %collective-permute-start.6 = (bf16[1040,128]{0,1:T(8,128)(2,1)S(1)}, bf16[1040,128]{0,1:T(8,128)(2,1)S(1)}, u32[]{:S(2)}, u32[]{:S(2)}) collective-permute-start(bf16[1040,128]{0,1:T(8,128)(2,1)S(1)} %pad_maximum_fusion.2), channel_id=1, source_target_pairs={{0,28},{1,29},{2,30},{3,31}} | collective-permute-start | bytes 798728 | tf_op jit(solution)/shard_map/ppermute | solution.py:17
  26.9 27.8 %copy-start.10 = (bf16[1040,128]{0,1:T(8,128)(2,1)}, bf16[1040,128]{0,1:T(8,128)(2,1)S(1)}, u32[]{:S(2)}) copy-start(bf16[1040,128]{0,1:T(8,128)(2,1)S(1)} %collective-permute-done.3) | copy-start | bytes 798724
  27.0 22.6 %collective-permute-start.5 = (bf16[1040,128]{0,1:T(8,128)(2,1)S(1)}, bf16[1040,128]{0,1:T(8,128)(2,1)S(1)}, u32[]{:S(2)}, u32[]{:S(2)}) collective-permute-start(bf16[1040,128]{0,1:T(8,128)(2,1)S(1)} %pad_maximum_fusion.2), channel_id=1, source_target_pairs={{0,24},{4,28},{1,25},{5,29},{2,26},{6,30},{3,27},{7,31}} | collective-permute-start | bytes 798728 | tf_op jit(solution)/shard_map/ppermute | solution.py:17
  35.6 19.1 %collective-permute-start.4 = (bf16[1040,128]{0,1:T(8,128)(2,1)S(1)}, bf16[1040,128]{0,1:T(8,128)(2,1)S(1)}, u32[]{:S(2)}, u32[]{:S(2)}) collective-permute-start(bf16[1040,128]{0,1:T(8,128)(2,1)S(1)} %pad_maximum_fusion.2), channel_id=1, source_target_pairs={{0,20},{4,24},{8,28},{1,21},{5,25},{9,29},{2,22},{6,26},{10,30},{3... | collective-permute-start | bytes 798728 | tf_op jit(solution)/shard_map/ppermute | solution.py:17
  80.6 25.1 %collective-permute-start.7 = (bf16[128,1024]{0,1:T(8,128)(2,1)S(1)}, bf16[128,1024]{0,1:T(8,128)(2,1)S(1)}, u32[]{:S(2)}, u32[]{:S(2)}) collective-permute-start(bf16[128,1024]{0,1:T(8,128)(2,1)S(1)} %bitcast.152), channel_id=1, source_target_pairs={{0,4},{4,8},{8,12},{12,16},{16,20},{20,24},{24,28},{28,0},{1,5},{5... | collective-permute-start | bytes 786440 | tf_op jit(solution)/shard_map/ppermute | solution.py:17
  83.0 23.2 %collective-permute-start.8 = (bf16[128,1024]{0,1:T(8,128)(2,1)S(1)}, bf16[128,1024]{0,1:T(8,128)(2,1)S(1)}, u32[]{:S(2)}, u32[]{:S(2)}) collective-permute-start(bf16[128,1024]{0,1:T(8,128)(2,1)S(1)} %bitcast.153), channel_id=1, source_target_pairs={{0,8},{4,12},{8,16},{12,20},{16,24},{20,28},{24,0},{28,4},{1,9},{5... | collective-permute-start | bytes 786440 | tf_op jit(solution)/shard_map/ppermute | solution.py:17
  96.5 31.0 %collective-permute-start.9 = (bf16[128,1024]{0,1:T(8,128)(2,1)S(1)}, bf16[128,1024]{0,1:T(8,128)(2,1)S(1)}, u32[]{:S(2)}, u32[]{:S(2)}) collective-permute-start(bf16[128,1024]{0,1:T(8,128)(2,1)S(1)} %bitcast.154), channel_id=1, source_target_pairs={{0,12},{4,16},{8,20},{12,24},{16,28},{20,0},{24,4},{28,8},{1,13},{... | collective-permute-start | bytes 786440 | tf_op jit(solution)/shard_map/ppermute | solution.py:17
  99.3 28.6 %collective-permute-start.10 = (bf16[128,1024]{0,1:T(8,128)(2,1)S(1)}, bf16[128,1024]{0,1:T(8,128)(2,1)S(1)}, u32[]{:S(2)}, u32[]{:S(2)}) collective-permute-start(bf16[128,1024]{0,1:T(8,128)(2,1)S(1)} %bitcast.155), channel_id=1, source_target_pairs={{0,16},{4,20},{8,24},{12,28},{16,0},{20,4},{24,8},{28,12},{1,17},{... | collective-permute-start | bytes 786440 | tf_op jit(solution)/shard_map/ppermute | solution.py:17
  100.0 28.4 %collective-permute-start.11 = (bf16[128,1024]{0,1:T(8,128)(2,1)S(1)}, bf16[128,1024]{0,1:T(8,128)(2,1)S(1)}, u32[]{:S(2)}, u32[]{:S(2)}) collective-permute-start(bf16[128,1024]{0,1:T(8,128)(2,1)S(1)} %bitcast.156), channel_id=1, source_target_pairs={{0,20},{4,24},{8,28},{12,0},{16,4},{20,8},{24,12},{28,16},{1,21},{... | collective-permute-start | bytes 786440 | tf_op jit(solution)/shard_map/ppermute | solution.py:17
  105.7 23.1 %collective-permute-start.12 = (bf16[128,1024]{0,1:T(8,128)(2,1)S(1)}, bf16[128,1024]{0,1:T(8,128)(2,1)S(1)}, u32[]{:S(2)}, u32[]{:S(2)}) collective-permute-start(bf16[128,1024]{0,1:T(8,128)(2,1)S(1)} %bitcast.158), channel_id=1, source_target_pairs={{0,24},{4,28},{8,0},{12,4},{16,8},{20,12},{24,16},{28,20},{1,25},{... | collective-permute-start | bytes 786440 | tf_op jit(solution)/shard_map/ppermute | solution.py:17
  106.2 23.9 %collective-permute-start.13 = (bf16[128,1024]{0,1:T(8,128)(2,1)S(1)}, bf16[128,1024]{0,1:T(8,128)(2,1)S(1)}, u32[]{:S(2)}, u32[]{:S(2)}) collective-permute-start(bf16[128,1024]{0,1:T(8,128)(2,1)S(1)} %bitcast.159), channel_id=1, source_target_pairs={{0,28},{4,0},{8,4},{12,8},{16,12},{20,16},{24,20},{28,24},{1,29},{... | collective-permute-start | bytes 786440 | tf_op jit(solution)/shard_map/ppermute | solution.py:17
  130.5 57.4 %copy-start.2 = (bf16[128,1536]{1,0:T(8,128)(2,1)S(1)}, bf16[128,1536]{1,0:T(8,128)(2,1)}, u32[]{:S(2)}) copy-start(bf16[128,1536]{1,0:T(8,128)(2,1)} %param.21) | copy-start | bytes 1179652
  131.7 124.8 %all-gather.3.cloned.1.call-start = ((), (), s32[]{:S(2)}) async-start(), calls=%async_computation.8 | async-start | bytes 3932160 | tf_op jit(solution)/shard_map/all_gather | solution.py:185
  176.2 7.3 %collective-permute-start.14 = (bf16[128,768]{1,0:T(8,128)(2,1)S(1)}, bf16[128,768]{1,0:T(8,128)(2,1)S(1)}, u32[]{:S(2)}, u32[]{:S(2)}) collective-permute-start(bf16[128,768]{1,0:T(8,128)(2,1)S(1)} %get-tuple-element.18), channel_id=1, source_target_pairs={{0,0},{1,24},{2,16},{3,8},{4,4},{5,28},{6,20},{7,12},{8,9},{9,1},{... | collective-permute-start | bytes 589832 | tf_op jit(solution)/shard_map/ppermute | solution.py:89
  176.9 10.9 %collective-permute-start.15 = (bf16[128,768]{1,0:T(8,128)(2,1)S(1)}, bf16[128,768]{1,0:T(8,128)(2,1)S(1)}, u32[]{:S(2)}, u32[]{:S(2)}) collective-permute-start(bf16[128,768]{1,0:T(8,128)(2,1)S(1)} %get-tuple-element.17), channel_id=1, source_target_pairs={{0,28},{1,20},{2,12},{3,4},{4,0},{5,24},{6,16},{7,8},{8,5},{9,29},... | collective-permute-start | bytes 589832 | tf_op jit(solution)/shard_map/ppermute | solution.py:89
  229.4 57.3 %all-gather.5.cloned.1.call-start = ((), (), s32[]{:S(2)}) async-start(), calls=%async_computation.10 | async-start | bytes 3932160 | tf_op jit(solution)/shard_map/all_gather | solution.py:185
  252.6 74.6 %reduce-scatter.6.cloned.1.call-start = ((), (), s32[]{:S(2)}) async-start(), calls=%async_computation.9 | async-start | bytes 3932160 | tf_op jit(solution)/shard_map/reduce_scatter | solution.py:190
  256.5 18.6 %slice-start = ((s8[14155776]{0:T(1024)(128)(4,1)}), s8[4194304]{0:T(1024)(128)(4,1)S(1)}, s32[]{:S(2)}) async-start(s8[14155776]{0:T(1024)(128)(4,1)} %bitcast.169), calls=%async_computation.12 | async-start | bytes 8388608
  256.5 18.6 %slice-start.1 = ((s8[14155776]{0:T(1024)(128)(4,1)}), s8[4194304]{0:T(1024)(128)(4,1)S(1)}, s32[]{:S(2)}) async-start(s8[14155776]{0:T(1024)(128)(4,1)} %bitcast.169), calls=%async_computation.13 | async-start | bytes 8388608
  256.5 18.6 %slice-start.2 = ((s8[14155776]{0:T(1024)(128)(4,1)}), s8[4194304]{0:T(1024)(128)(4,1)S(1)}, s32[]{:S(2)}) async-start(s8[14155776]{0:T(1024)(128)(4,1)} %bitcast.169), calls=%async_computation.14 | async-start | bytes 8388608
  280.9 86.7 %reduce-scatter.8.cloned.1.call-start = ((), (), s32[]{:S(2)}) async-start(), calls=%async_computation.11 | async-start | bytes 3932160 | tf_op jit(solution)/shard_map/reduce_scatter | solution.py:190
  286.7 19.1 %slice-start.4 = ((s8[14155776]{0:T(1024)(128)(4,1)}), s8[4194304]{0:T(1024)(128)(4,1)S(1)}, s32[]{:S(2)}) async-start(s8[14155776]{0:T(1024)(128)(4,1)} %bitcast.171), calls=%async_computation.16 | async-start | bytes 8388608
  286.7 19.1 %slice-start.5 = ((s8[14155776]{0:T(1024)(128)(4,1)}), s8[4194304]{0:T(1024)(128)(4,1)S(1)}, s32[]{:S(2)}) async-start(s8[14155776]{0:T(1024)(128)(4,1)} %bitcast.171), calls=%async_computation.17 | async-start | bytes 8388608
  286.7 19.2 %slice-start.6 = ((s8[14155776]{0:T(1024)(128)(4,1)}), s8[4194304]{0:T(1024)(128)(4,1)S(1)}, s32[]{:S(2)}) async-start(s8[14155776]{0:T(1024)(128)(4,1)} %bitcast.171), calls=%async_computation.18 | async-start | bytes 8388608
  327.3 40.3 %all-to-all-start.1 = ((bf16[8,32,1536]{2,1,0:T(8,128)(2,1)}), bf16[8,32,1536]{2,1,0:T(8,128)(2,1)S(1)}, u32[]{:S(2)}, u32[]{:S(2)}) async-start(bf16[8,32,1536]{2,1,0:T(8,128)(2,1)} %bitcast.161), calls=%async_computation.3 | async-start | bytes 1572864 | tf_op jit(solution)/shard_map/all_to_all | solution.py:195
  367.6 25.7 %all-to-all-start.3 = ((bf16[8,32,1536]{2,1,0:T(8,128)(2,1)}), bf16[8,32,1536]{2,1,0:T(8,128)(2,1)S(1)}, u32[]{:S(2)}, u32[]{:S(2)}) async-start(bf16[8,32,1536]{2,1,0:T(8,128)(2,1)} %bitcast.160), calls=%async_computation.6 | async-start | bytes 1572864 | tf_op jit(solution)/shard_map/all_to_all | solution.py:195
  (17 other events, 123.0 us)
Sparse Core Ops, SparseCore 0:
  131.8 43.2 reduce-scatter.3
  229.5 26.9 all-gather.2
  258.2 28.5 all-gather.4
  289.3 37.9 reduce-scatter.5
  329.7 37.9 reduce-scatter.7

commit v5 on v3

--- a/solution.py
+++ b/solution.py
@@ -60,6 +60,27 @@
     return (earlier[0] + latter[0], jnp.exp(latter[0])[:, None, None] * earlier[1] + latter[1])
 
 
+def head_sum(partial, axis):
+    size, place = (lax.axis_size("head"), lax.axis_index("head"))
+    chips, chip, core = (size // 2, place // 2, place % 2)
+    width = partial.shape[axis] // size
+    swap = [(h, h ^ 1) for h in range(size)]
+
+    def piece(owner):
+        return lax.dynamic_slice_in_dim(partial, owner * width, width, axis)
+
+    total = None
+    for turn in range(chips - 1, -1, -1):
+        to = (chip + turn) % chips
+        got = lax.ppermute(piece(2 * to + 1 - core), "head", swap)
+        both = piece(2 * to + core).astype(jnp.float32) + got.astype(jnp.float32)
+        if turn:
+            pairs = [(h, (h + 2 * turn) % size) for h in range(size)]
+            both = lax.ppermute(both.astype(jnp.bfloat16), "head", pairs).astype(jnp.float32)
+        total = both if total is None else total + both
+    return total.astype(jnp.bfloat16)
+
+
 def project(attn_rows, out_weight):
     seq_size, head_size = (lax.axis_size("seq"), lax.axis_size("head"))
     place = lax.axis_index("seq")
@@ -67,9 +88,7 @@
     ratio = seq_size // head_size
     all_rows = lax.all_gather(attn_rows, "seq", axis=0, tiled=True)
     products = jnp.dot(all_rows, out_weight, preferred_element_type=jnp.float32)
-    sums = lax.psum_scatter(
-        products.astype(jnp.bfloat16), "head", scatter_dimension=0, tiled=True
-    ).reshape(ratio, tokens_here, -1)
+    sums = head_sum(products.astype(jnp.bfloat16), 0).reshape(ratio, tokens_here, -1)
     landed = []
     for turn in range(ratio):
         pairs = [
@@ -180,9 +199,7 @@
         up_act = jnp.dot(portion, up_here, preferred_element_type=jnp.float32)
         hidden = (jax.nn.silu(gate_act) * up_act).astype(jnp.bfloat16)
         partial_value = jnp.dot(hidden, down_here, preferred_element_type=jnp.float32)
-        summed = lax.psum_scatter(
-            partial_value.astype(jnp.bfloat16), "head", scatter_dimension=1, tiled=True
-        )
+        summed = head_sum(partial_value.astype(jnp.bfloat16), 1)
         returning = summed.reshape(experts, chunk, -1)
         results.append(
             lax.all_to_all(returning, "seq", split_axis=0, concat_axis=0, tiled=True)

time: 397 us -> 369 us (0.929)
  waiting for transfers between devices: 185 us -> 146 us
  other arithmetic: 16.4 us -> 25.5 us
  local copies, waits for them, and re-layouts: 13.2 us -> 17.9 us
  matrix products: 60 us -> 55.6 us
    reduce_scatter x3 -> x0, waiting for transfers between devices: 76.3 us -> none  [the longest x2 50.6 us: on_device(): lax.psum_scatter(partial_value.astype(jnp.bfloat16), 'head', scatter_dime...]
    ppermute x0 -> x9, waiting for transfers between devices: none -> 39.4 us  [the longest x3 38.7 us: head_sum(): lax.ppermute(both.astype(jnp.bfloat16), 'head', pairs).astype(jnp.float32)]
    convert_element_type x0 -> x6, other arithmetic: none -> 9.19 us  [the longest x3 5.24 us: head_sum(): return total.astype(jnp.bfloat16)]
  transfers between devices with their start and end apart: 11 -> 17, of which waited for: 9 -> 10; matrix products, arithmetic and copies ran while one was open for 13% -> 17% of each run, Pallas kernels for 0% -> 0%
where the time goes in v5:
time: 369 us; the launch traced here: 368 us
  waiting for transfers between devices  146 us (40%)
  blocking collectives  90.6 us (25%)
  matrix products  55.6 us (15%)
  other arithmetic  25.5 us (7%)
  local copies, waits for them, and re-layouts  17.9 us (5%)
  starting transfers between devices  17.2 us (5%)
  between operations  14.5 us (4%)
    all_gather x1, waiting for transfers between devices, project(): all_rows = lax.all_gather(attn_rows, 'seq', axis=0, tiled=True)  49.6 us
    all_to_all x2, blocking collectives, on_device(): lax.all_to_all(outgoing[:, c * chunk:(c + 1) * chunk], 'seq', split_axis=...  47.2 us
    ppermute x3, waiting for transfers between devices, head_sum(): lax.ppermute(both.astype(jnp.bfloat16), 'head', pairs).astype(jnp.float32)  38.7 us
    all_gather x1, waiting for transfers between devices, prefix(): lax.all_gather(part.astype(kind), axis)  27.1 us
    unnamed x1, blocking collectives  23.1 us
    dot_general x2, matrix products, on_device(): gate_act = jnp.dot(portion, gate_here, preferred_element_type=jnp.float32)  21.1 us
    psum x1, blocking collectives, on_device(): lax.psum((jnp.sum(stream_here * stream_here, axis=-1), jnp.dot(weighted,...  20.3 us
    all_to_all x2, waiting for transfers between devices, on_device(): lax.all_to_all(returning, 'seq', split_axis=0, concat_axis=0, tiled=True)  17.3 us
  transfers between devices with their start and end apart: 17, of which 10 were waited for; matrix products, arithmetic and copies ran while one was open for 17% of the time, Pallas kernels for 0%

profile of v5, /device:TPU:0, one launch (start us, length us, event | category | flops | bytes accessed | tf_op | source)
XLA Modules:
  0.0 367.8 jit_solution(10655184699498253654)
XLA Ops:
  13.1 23.1 %all-reduce = bf16[64]{0:T(256)(128)(2,1)S(1)} all-reduce(bf16[64]{0:T(256)(128)(2,1)S(1)} %dynamic-update-slice), channel_id=2, replica_groups=mesh['seq'=8,'head'=4] {'seq'}, use_global_device_ids=true, to_apply=%add | all-reduce | flops 64 | bytes 256
  36.3 27.1 %all-gather.13.cloned.1.call-done = bf16[64,128,128]{2,1,0:T(8,128)(2,1)} async-done(((bf16[8,128,128]{2,1,0:T(8,128)(2,1)}), bf16[64,128,128]{2,1,0:T(8,128)(2,1)}) %all-gather.13.cloned.1.call-update) | async-done | bytes 2097168 | tf_op jit(solution)/shard_map/all_gather | solution.py:18
  63.5 9.1 %while.16 = (s32[]{:T(128)}, f32[8]{0:T(128)S(1)}, f32[8,128,128]{2,1,0:T(8,128)S(1)}, s32[]{:T(128)}, bf16[8,8]{1,0:T(8,128)(2,1)S(1)}, /*index=5*/bf16[8,8,128,128]{3,2,1,0:T(8,128)(2,1)}, s32[]{:T(128)}, s32[]{:T(128)}) while((s32[]{:T(128)}, f32[8]{0:T(128)S(1)}, f32[8,128,128]{2,1,0:T(8,128)S(1)}, s32[]{:T(128)}, ...), condition=%wide.region_2.3_spmd.clone, body=%wide.region_1.2_spmd.clone.sunk | while | flops 655396 | bytes 1310979 | solution.py:31
  72.6 1.6 fusion.32
  76.9 49.6 %all-gather.7.cloned.1.call-done = bf16[1024,1024]{0,1:T(8,128)(2,1)} async-done(((bf16[128,1024]{0,1:T(8,128)(2,1)}), bf16[1024,1024]{0,1:T(8,128)(2,1)}) %all-gather.7.cloned.1.call-update) | async-done | bytes 2097168 | tf_op jit(solution)/shard_map/all_gather | solution.py:89
  126.5 3.4 convolution_convert_fusion
  134.0 9.1 %collective-permute-done.1 = bf16[256,768]{1,0:T(8,128)(2,1)S(1)} collective-permute-done((bf16[256,768]{1,0:T(8,128)(2,1)S(1)}, bf16[256,768]{1,0:T(8,128)(2,1)S(1)}, u32[]{:S(2)}, u32[]{:S(2)}) %collective-permute-start.1) | collective-permute-done | bytes 393248 | tf_op jit(solution)/shard_map/ppermute | solution.py:79
  146.6 3.2 collective-permute-done.4
  151.7 20.3 %all-reduce.1 = (f32[128]{0:T(128)S(1)}, f32[128,8]{0,1:T(8,128)S(1)}) all-reduce(f32[128]{0:T(128)S(1)} %multiply_reduce_fusion.1, f32[128,8]{0,1:T(8,128)S(1)} %fusion.35), channel_id=1, replica_groups=mesh['seq'=8,'head'=4] {'head'}, use_global_device_ids=true, to_apply=%region_6.7 | all-reduce | flops 1152 | bytes 9216 | tf_op jit(solution)/shard_map/psum | solution.py:154
  172.7 2.1 gather_fusion
  175.2 24.0 %all_to_all.20 = bf16[8,32,1536]{2,1,0:T(8,128)(2,1)} all-to-all(bf16[8,32,1536]{2,1,0:T(8,128)(2,1)S(1)} %get-tuple-element.170), channel_id=1, replica_groups=mesh['seq'=8,'head'=4] {'seq'}, dimensions={0} | all-to-all | bytes 1572864 | tf_op jit(solution)/shard_map/all_to_all | solution.py:185
  199.3 23.2 %all_to_all.21 = bf16[8,32,1536]{2,1,0:T(8,128)(2,1)} all-to-all(bf16[8,32,1536]{2,1,0:T(8,128)(2,1)S(1)} %get-tuple-element.171), channel_id=1, replica_groups=mesh['seq'=8,'head'=4] {'seq'}, dimensions={0} | all-to-all | bytes 1572864 | tf_op jit(solution)/shard_map/all_to_all | solution.py:185
  222.5 4.6 %all-gather.9.cloned.1.call-done = bf16[256,6144]{1,0:T(8,128)(2,1)} async-done(((bf16[256,1536]{1,0:T(8,128)(2,1)}), bf16[256,6144]{1,0:T(8,128)(2,1)}) %all-gather.9.cloned.1.call-update) | async-done | bytes 3145744 | tf_op jit(solution)/shard_map/all_gather | solution.py:197
  227.1 10.7 %fusion.11 = f32[256,1152]{1,0:T(8,128)S(1)} fusion(bf16[256,6144]{1,0:T(8,128)(2,1)} %all-gather.9.cloned.1.call-done, bf16[1,6144,1152]{2,1,0:T(8,128)(2,1)} %param.27), kind=kOutput, calls=%fused_computation.18 | convolution fusion | flops 3623878656 | bytes 18481152 | tf_op jit(solution)/shard_map/dot_general | solution.py:198
  237.9 8.0 %fusion.28 = bf16[256,1152]{1,0:T(8,128)(2,1)S(1)} fusion(bf16[256,6144]{1,0:T(8,128)(2,1)S(1)} %copy-done.16, bf16[1,6144,1152]{2,1,0:T(8,128)(2,1)} %param.28, f32[256,1152]{1,0:T(8,128)S(1)} %fusion.11), kind=kOutput, calls=%fused_computation.25 | convolution fusion | flops 3625648128 | bytes 19070976 | tf_op jit(solution)/shard_map/dot_general | solution.py:199
  245.9 4.4 %fusion.13 = bf16[256,6144]{1,0:T(8,128)(2,1)S(1)} fusion(bf16[256,1152]{1,0:T(8,128)(2,1)S(1)} %fusion.28, bf16[1,1152,6144]{2,1,0:T(8,128)(2,1)S(1)} %bitcast.137), kind=kOutput, calls=%fused_computation.20 | convolution fusion | flops 3625451520 | bytes 17891328 | tf_op jit(solution)/shard_map/dot_general | solution.py:201
  252.1 4.9 %all-gather.11.cloned.1.call-done = bf16[256,6144]{1,0:T(8,128)(2,1)} async-done(((bf16[256,1536]{1,0:T(8,128)(2,1)}), bf16[256,6144]{1,0:T(8,128)(2,1)}) %all-gather.11.cloned.1.call-update) | async-done | bytes 3145744 | tf_op jit(solution)/shard_map/all_gather | solution.py:197
  257.1 10.3 %fusion.9 = f32[256,1152]{1,0:T(8,128)S(1)} fusion(bf16[256,6144]{1,0:T(8,128)(2,1)} %all-gather.11.cloned.1.call-done, bf16[1,6144,1152]{2,1,0:T(8,128)(2,1)} %param.27), kind=kOutput, calls=%fused_computation.16 | convolution fusion | flops 3623878656 | bytes 18481152 | tf_op jit(solution)/shard_map/dot_general | solution.py:198
  267.4 8.0 %fusion.25 = bf16[256,1152]{1,0:T(8,128)(2,1)S(1)} fusion(bf16[256,6144]{1,0:T(8,128)(2,1)S(1)} %copy-done.15, bf16[1,6144,1152]{2,1,0:T(8,128)(2,1)} %param.28, f32[256,1152]{1,0:T(8,128)S(1)} %fusion.9), kind=kOutput, calls=%fused_computation.24 | convolution fusion | flops 3625648128 | bytes 19070976 | tf_op jit(solution)/shard_map/dot_general | solution.py:199
  275.4 2.3 add_convert_fusion.3
  278.0 4.7 %fusion.16 = bf16[256,6144]{1,0:T(8,128)(2,1)S(1)} fusion(bf16[256,1152]{1,0:T(8,128)(2,1)S(1)} %fusion.25, bf16[1,1152,6144]{2,1,0:T(8,128)(2,1)S(1)} %bitcast.139), kind=kOutput, calls=%fused_computation.21 | convolution fusion | flops 3625451520 | bytes 17891328 | tf_op jit(solution)/shard_map/dot_general | solution.py:201
  282.7 1.6 copy-done.3
  286.2 11.6 %collective-permute-done.6 = bf16[256,1536]{1,0:T(8,128)(2,1)} collective-permute-done((bf16[256,1536]{1,0:T(8,128)(2,1)}, bf16[256,1536]{1,0:T(8,128)(2,1)}, u32[]{:S(2)}, u32[]{:S(2)}) %collective-permute-start.6) | collective-permute-done | bytes 786464 | tf_op jit(solution)/shard_map/ppermute | solution.py:79
  297.7 2.6 add_convert_fusion.2
  300.3 5.5 %all-to-all-start.1 = ((bf16[8,32,1536]{2,1,0:T(8,128)(2,1)}), bf16[8,32,1536]{2,1,0:T(8,128)(2,1)S(1)}, u32[]{:S(2)}, u32[]{:S(2)}) async-start(bf16[8,32,1536]{2,1,0:T(8,128)(2,1)} %bitcast.123), calls=%async_computation.1 | async-start | bytes 1572864 | tf_op jit(solution)/shard_map/all_to_all | solution.py:205
  308.0 18.1 %collective-permute-done.9 = bf16[256,1536]{1,0:T(8,128)(2,1)S(1)} collective-permute-done((bf16[256,1536]{1,0:T(8,128)(2,1)S(1)}, bf16[256,1536]{1,0:T(8,128)(2,1)S(1)}, u32[]{:S(2)}, u32[]{:S(2)}) %collective-permute-start.9) | collective-permute-done | bytes 786464 | tf_op jit(solution)/shard_map/ppermute | solution.py:79
  326.1 2.5 add_convert_fusion
  328.6 5.7 %all-to-all-start.3 = ((bf16[8,32,1536]{2,1,0:T(8,128)(2,1)}), bf16[8,32,1536]{2,1,0:T(8,128)(2,1)S(1)}, u32[]{:S(2)}, u32[]{:S(2)}) async-start(bf16[8,32,1536]{2,1,0:T(8,128)(2,1)} %bitcast.25), calls=%async_computation.3 | async-start | bytes 1572864 | tf_op jit(solution)/shard_map/all_to_all | solution.py:205
  335.4 17.3 %all-to-all-done.3 = bf16[8,32,1536]{2,1,0:T(8,128)(2,1)S(1)} async-done(((bf16[8,32,1536]{2,1,0:T(8,128)(2,1)}), bf16[8,32,1536]{2,1,0:T(8,128)(2,1)S(1)}, u32[]{:S(2)}, u32[]{:S(2)}) %all-to-all-start.3) | async-done | bytes 786464 | tf_op jit(solution)/shard_map/all_to_all | solution.py:205
  352.8 2.1 gather_fusion.1
  355.0 2.2 reshape.197
  357.2 3.2 multiply_reduce_fusion
  (150 shorter events, 36.0 us)
Async XLA Ops:
  6.5 119.9 %copy-start = (bf16[1024,768]{1,0:T(8,128)(2,1)S(1)}, bf16[1024,768]{1,0:T(8,128)(2,1)}, u32[]{:S(2)}) copy-start(bf16[1024,768]{1,0:T(8,128)(2,1)} %param.22) | copy-start | bytes 4718596
  6.5 56.9 %all-gather.13.cloned.1.call-start = ((), (), s32[]{:S(2)}) async-start(), calls=%async_computation.7 | async-start | bytes 2359296 | tf_op jit(solution)/shard_map/all_gather | solution.py:18
  11.2 115.3 %all-gather.7.cloned.1.call-start = ((), (), s32[]{:S(2)}) async-start(), calls=%async_computation.4 | async-start | bytes 2359296 | tf_op jit(solution)/shard_map/all_gather | solution.py:89
  63.5 9.2 %copy-start.8 = (f32[8,128,128]{2,1,0:T(8,128)S(1)}, f32[8,128,128]{2,1,0:T(8,128)}, u32[]{:S(2)}) copy-start(f32[8,128,128]{2,1,0:T(8,128)} %param.20) | copy-start | bytes 1572868
  76.8 150.3 %all-gather.9.cloned.1.call-start = ((), (), s32[]{:S(2)}) async-start(), calls=%async_computation.5 | async-start | bytes 3932160 | tf_op jit(solution)/shard_map/all_gather | solution.py:197
  130.0 1.8 collective-permute-start
  131.1 3.0 collective-permute-start.2
  131.9 11.2 %collective-permute-start.1 = (bf16[256,768]{1,0:T(8,128)(2,1)S(1)}, bf16[256,768]{1,0:T(8,128)(2,1)S(1)}, u32[]{:S(2)}, u32[]{:S(2)}) collective-permute-start(bf16[256,768]{1,0:T(8,128)(2,1)S(1)} %add_convert_fusion.6), channel_id=1, source_target_pairs={{0,2},{1,3},{2,0},{3,1},{4,6},{5,7},{6,4},{7,5},{8,10},{9,11},{10,... | collective-permute-start | bytes 1179656 | tf_op jit(solution)/shard_map/ppermute | solution.py:79
  134.0 11.5 %copy-start.12 = (s32[256]{0:T(256)S(1)}, s32[256]{0:T(256)}, u32[]{:S(2)}) copy-start(s32[256]{0:T(256)} %copy-done.11) | copy-start | bytes 3076
  134.0 15.9 %copy-start.2 = (bf16[128,1536]{1,0:T(8,128)(2,1)S(1)}, bf16[128,1536]{1,0:T(8,128)(2,1)}, u32[]{:S(2)}) copy-start(bf16[128,1536]{1,0:T(8,128)(2,1)} %param.23) | copy-start | bytes 1179652
  143.3 3.2 collective-permute-start.3
  144.0 5.7 %collective-permute-start.4 = (bf16[128,768]{1,0:T(8,128)(2,1)S(1)}, bf16[128,768]{1,0:T(8,128)(2,1)S(1)}, u32[]{:S(2)}, u32[]{:S(2)}) collective-permute-start(bf16[128,768]{1,0:T(8,128)(2,1)S(1)} %get-tuple-element.176), channel_id=1, source_target_pairs={{0,4},{1,12},{2,20},{3,28},{4,0},{5,8},{6,16},{7,24},{8,5},{9,13},... | collective-permute-start | bytes 589832 | tf_op jit(solution)/shard_map/ppermute | solution.py:100
  149.9 22.1 %copy-start.4 = (bf16[128,768]{1,0:T(8,128)(2,1)}, bf16[128,768]{1,0:T(8,128)(2,1)S(1)}, u32[]{:S(2)}) copy-start(bf16[128,768]{1,0:T(8,128)(2,1)S(1)} %get-tuple-element.174) | copy-start | bytes 589828
  149.9 22.1 %copy-start.6 = (bf16[128,768]{1,0:T(8,128)(2,1)}, bf16[128,768]{1,0:T(8,128)(2,1)S(1)}, u32[]{:S(2)}) copy-start(bf16[128,768]{1,0:T(8,128)(2,1)S(1)} %get-tuple-element.175) | copy-start | bytes 589828
  199.2 57.8 %all-gather.11.cloned.1.call-start = ((), (), s32[]{:S(2)}) async-start(), calls=%async_computation.6 | async-start | bytes 3932160 | tf_op jit(solution)/shard_map/all_gather | solution.py:197
  227.1 10.8 %copy-start.16 = (bf16[256,6144]{1,0:T(8,128)(2,1)S(1)}, bf16[256,6144]{1,0:T(8,128)(2,1)}, u32[]{:S(2)}) copy-start(bf16[256,6144]{1,0:T(8,128)(2,1)} %all-gather.9.cloned.1.call-done) | copy-start | bytes 9437188
  227.1 18.8 %slice-start = ((s8[14155776]{0:T(1024)(128)(4,1)}), s8[4194304]{0:T(1024)(128)(4,1)S(1)}, s32[]{:S(2)}) async-start(s8[14155776]{0:T(1024)(128)(4,1)} %bitcast.136), calls=%async_computation.8 | async-start | bytes 8388608
  227.1 18.8 %slice-start.1 = ((s8[14155776]{0:T(1024)(128)(4,1)}), s8[4194304]{0:T(1024)(128)(4,1)S(1)}, s32[]{:S(2)}) async-start(s8[14155776]{0:T(1024)(128)(4,1)} %bitcast.136), calls=%async_computation.9 | async-start | bytes 8388608
  227.1 18.8 %slice-start.2 = ((s8[14155776]{0:T(1024)(128)(4,1)}), s8[4194304]{0:T(1024)(128)(4,1)S(1)}, s32[]{:S(2)}) async-start(s8[14155776]{0:T(1024)(128)(4,1)} %bitcast.136), calls=%async_computation.10 | async-start | bytes 8388608
  251.6 23.8 %collective-permute-start.5 = (bf16[256,1536]{1,0:T(8,128)(2,1)}, bf16[256,1536]{1,0:T(8,128)(2,1)}, u32[]{:S(2)}, u32[]{:S(2)}) collective-permute-start(bf16[256,1536]{1,0:T(8,128)(2,1)} %get-tuple-element.166), channel_id=1, source_target_pairs={{0,1},{1,0},{2,3},{3,2},{4,5},{5,4},{6,7},{7,6},{8,9},{9,8},{10,11... | collective-permute-start | bytes 2359304 | tf_op jit(solution)/shard_map/ppermute | solution.py:75
  251.8 34.4 %collective-permute-start.7 = (bf16[256,1536]{1,0:T(8,128)(2,1)}, bf16[256,1536]{1,0:T(8,128)(2,1)}, u32[]{:S(2)}, u32[]{:S(2)}) collective-permute-start(bf16[256,1536]{1,0:T(8,128)(2,1)} %get-tuple-element.167), channel_id=1, source_target_pairs={{0,1},{1,0},{2,3},{3,2},{4,5},{5,4},{6,7},{7,6},{8,9},{9,8},{10,11... | collective-permute-start | bytes 2359304 | tf_op jit(solution)/shard_map/ppermute | solution.py:75
  257.1 10.3 %copy-start.15 = (bf16[256,6144]{1,0:T(8,128)(2,1)S(1)}, bf16[256,6144]{1,0:T(8,128)(2,1)}, u32[]{:S(2)}) copy-start(bf16[256,6144]{1,0:T(8,128)(2,1)} %all-gather.11.cloned.1.call-done) | copy-start | bytes 9437188
  257.1 21.0 %slice-start.4 = ((s8[14155776]{0:T(1024)(128)(4,1)}), s8[4194304]{0:T(1024)(128)(4,1)S(1)}, s32[]{:S(2)}) async-start(s8[14155776]{0:T(1024)(128)(4,1)} %bitcast.138), calls=%async_computation.12 | async-start | bytes 8388608
  257.1 21.0 %slice-start.5 = ((s8[14155776]{0:T(1024)(128)(4,1)}), s8[4194304]{0:T(1024)(128)(4,1)S(1)}, s32[]{:S(2)}) async-start(s8[14155776]{0:T(1024)(128)(4,1)} %bitcast.138), calls=%async_computation.13 | async-start | bytes 8388608
  267.4 10.6 %slice-start.6 = ((s8[14155776]{0:T(1024)(128)(4,1)}), s8[4194304]{0:T(1024)(128)(4,1)S(1)}, s32[]{:S(2)}) async-start(s8[14155776]{0:T(1024)(128)(4,1)} %bitcast.138), calls=%async_computation.14 | async-start | bytes 8388608
  267.4 10.6 %slice-start.7 = ((s8[14155776]{0:T(1024)(128)(4,1)}), s8[1572864]{0:T(1024)(128)(4,1)S(1)}, s32[]{:S(2)}) async-start(s8[14155776]{0:T(1024)(128)(4,1)} %bitcast.138), calls=%async_computation.15 | async-start | bytes 3145728
  277.7 20.0 %collective-permute-start.6 = (bf16[256,1536]{1,0:T(8,128)(2,1)}, bf16[256,1536]{1,0:T(8,128)(2,1)}, u32[]{:S(2)}, u32[]{:S(2)}) collective-permute-start(bf16[256,1536]{1,0:T(8,128)(2,1)} %add_convert_fusion.3), channel_id=1, source_target_pairs={{0,2},{1,3},{2,0},{3,1},{4,6},{5,7},{6,4},{7,5},{8,10},{9,11},{10,... | collective-permute-start | bytes 2359304 | tf_op jit(solution)/shard_map/ppermute | solution.py:79
  285.7 20.1 %collective-permute-start.8 = (bf16[256,1536]{1,0:T(8,128)(2,1)}, bf16[256,1536]{1,0:T(8,128)(2,1)}, u32[]{:S(2)}, u32[]{:S(2)}) collective-permute-start(bf16[256,1536]{1,0:T(8,128)(2,1)} %get-tuple-element.168), channel_id=1, source_target_pairs={{0,1},{1,0},{2,3},{3,2},{4,5},{5,4},{6,7},{7,6},{8,9},{9,8},{10,11... | collective-permute-start | bytes 2359304 | tf_op jit(solution)/shard_map/ppermute | solution.py:75
  285.7 22.3 %collective-permute-start.10 = (bf16[256,1536]{1,0:T(8,128)(2,1)}, bf16[256,1536]{1,0:T(8,128)(2,1)}, u32[]{:S(2)}, u32[]{:S(2)}) collective-permute-start(bf16[256,1536]{1,0:T(8,128)(2,1)} %get-tuple-element.169), channel_id=1, source_target_pairs={{0,1},{1,0},{2,3},{3,2},{4,5},{5,4},{6,7},{7,6},{8,9},{9,8},{10,11... | collective-permute-start | bytes 2359304 | tf_op jit(solution)/shard_map/ppermute | solution.py:75
  300.3 28.3 %all-to-all-start.1 = ((bf16[8,32,1536]{2,1,0:T(8,128)(2,1)}), bf16[8,32,1536]{2,1,0:T(8,128)(2,1)S(1)}, u32[]{:S(2)}, u32[]{:S(2)}) async-start(bf16[8,32,1536]{2,1,0:T(8,128)(2,1)} %bitcast.123), calls=%async_computation.1 | async-start | bytes 1572864 | tf_op jit(solution)/shard_map/all_to_all | solution.py:205
  307.4 18.7 %collective-permute-start.9 = (bf16[256,1536]{1,0:T(8,128)(2,1)S(1)}, bf16[256,1536]{1,0:T(8,128)(2,1)S(1)}, u32[]{:S(2)}, u32[]{:S(2)}) collective-permute-start(bf16[256,1536]{1,0:T(8,128)(2,1)S(1)} %add_convert_fusion.1), channel_id=1, source_target_pairs={{0,2},{1,3},{2,0},{3,1},{4,6},{5,7},{6,4},{7,5},{8,10},{9,11},{10,... | collective-permute-start | bytes 2359304 | tf_op jit(solution)/shard_map/ppermute | solution.py:79
  328.6 24.1 %all-to-all-start.3 = ((bf16[8,32,1536]{2,1,0:T(8,128)(2,1)}), bf16[8,32,1536]{2,1,0:T(8,128)(2,1)S(1)}, u32[]{:S(2)}, u32[]{:S(2)}) async-start(bf16[8,32,1536]{2,1,0:T(8,128)(2,1)} %bitcast.25), calls=%async_computation.3 | async-start | bytes 1572864 | tf_op jit(solution)/shard_map/all_to_all | solution.py:205
  (11 other events, 34.3 us)
Sparse Core Ops, SparseCore 0:
  11.3 52.0 all-gather.12
  76.9 49.5 all-gather.6
  199.4 27.6 all-gather.8
  228.5 28.5 all-gather.10
